TPU v7x, 256 devices: a whole 4x4x8 slice. The times are simulated.
256 devices in a mesh: shots: 32 (over z, y_hi, core), depth: 8 (over x, y_lo).
Axes of the slice: x: 4, y: 4 (y_hi: 2, y_lo: 2; y = y_hi * 2 + y_lo), z: 8, core: 2. Of those that a mesh axis runs over, the one named last changes fastest.
Arguments:
- model: float32 [32, 512, 512], P('depth', 'shots'), may hold values from 1.5 to 4.5
- offsets_x: int32 [32], replicated, may hold values from 0 to 448
- offsets_y: int32 [32], replicated, may hold values from 0 to 256
- ckpt_prev: float32 [32, 32, 64, 256], P('shots', 'depth'), may hold values from -6 to 6
- ckpt_cur: float32 [32, 32, 64, 256], P('shots', 'depth'), may hold values from -6 to 6
- wavelet: float32 [32, 4], P('shots'), may hold values from -128 to 128
- source: int32 [32], P('shots'), may hold values from 0 to 524287
- receivers: int32 [32, 4096], P('shots'), may hold values from 0 to 524287
- traces: float32 [32, 4, 4096], P('shots'), may hold values from -6 to 6
Outputs:
- gradient: float32 [32, 512, 512], P('depth', 'shots')
All inputs are finite; a program needn't handle non-finite values.
Results may differ from a plain program's by a relative error of at most 0.0003.
Values sent between devices are 32-bit elements; how exact they have to be, the bound alone decides.
A program may use at most 64 MiB of HBM per device.

v0:
```python
import jax
import jax.numpy as jnp
from jax import lax
from jax.sharding import PartitionSpec as P

STEPS = 4


stencil_weights = (-205.0 / 72.0, 8.0 / 5.0, -1.0 / 5.0, 8.0 / 315.0, -1.0 / 560.0)
courant = 0.095
lower_bound = 1.0
upper_bound = 5.0
barrier_weight = 0.5


def padded_2(shard, sides, width):
    for axis, dim in sides:
        devices, length = (lax.axis_size(axis), shard.shape[dim])
        up = [(i, (i + 1) % devices) for i in range(devices - 1)]
        down = [(j, i) for i, j in up]
        last = lax.slice_in_dim(shard, length - width, length, axis=dim)
        first = lax.slice_in_dim(shard, 0, width, axis=dim)
        before = lax.ppermute(last, axis, up)
        after = lax.ppermute(first, axis, down)
        shard = jnp.concatenate([before, shard, after], axis=dim)
    return shard


def laplace(field):
    depth_n, rows_n, cols_n = field.shape
    extended = padded_2(field, (("depth", 0),), 4)
    padded = jnp.pad(extended, ((0, 0), (4, 4), (4, 4)))
    total = 3.0 * stencil_weights[0] * field
    for step in range(1, 5):
        part = padded[4 + step : 4 + step + depth_n, 4 : 4 + rows_n, 4 : 4 + cols_n]
        part = part + padded[4 - step : 4 - step + depth_n, 4 : 4 + rows_n, 4 : 4 + cols_n]
        part = part + padded[4 : 4 + depth_n, 4 + step : 4 + step + rows_n, 4 : 4 + cols_n]
        part = part + padded[4 : 4 + depth_n, 4 - step : 4 - step + rows_n, 4 : 4 + cols_n]
        part = part + padded[4 : 4 + depth_n, 4 : 4 + rows_n, 4 + step : 4 + step + cols_n]
        part = part + padded[4 : 4 + depth_n, 4 : 4 + rows_n, 4 - step : 4 - step + cols_n]
        total = total + stencil_weights[step] * part
    return total


def inject_local(field, places, values, level):
    plane = field.shape[1] * field.shape[2]
    first = level * field.shape[0] * plane
    inside = (places >= first) & (places < first + field.shape[0] * plane)
    local_places = jnp.where(inside, places - first, 0)
    local_values = jnp.where(inside, values, 0.0)
    return field.reshape(-1).at[local_places].add(local_values).reshape(field.shape)


def on_device(model, offsets_x, offsets_y, ckpt_prev, ckpt_cur, wavelet, source, receivers, traces):
    slab_depth, rows_own, width_y = model.shape
    group = lax.axis_index("shots")
    level = lax.axis_index("depth")
    prev = ckpt_prev[0]
    cur = ckpt_cur[0]
    span_x, span_y = (cur.shape[1], cur.shape[2])
    own_x = offsets_x[group]
    own_y = offsets_y[group]
    highest = lax.Precision.HIGHEST
    piece = lax.all_gather(model, "shots", axis=1, tiled=True)
    cropped = lax.dynamic_slice_in_dim(piece, own_y, span_y, 2)
    rows = jnp.arange(piece.shape[1], dtype=jnp.int32)
    wanted = own_x + jnp.arange(span_x, dtype=jnp.int32)
    select = (wanted[:, None] == rows[None, :]).astype(jnp.float32)
    speed = jnp.einsum("xj,zjy->zxy", select, cropped, precision=highest)
    c2v = (courant * speed) ** 2
    place = source[0]
    listing = receivers[0]
    record = traces[0]
    pulse = wavelet[0]
    accels = []
    for step in range(STEPS):
        accel = inject_local(c2v * laplace(cur), place[None], pulse[step][None], level)
        accels.append(accel)
        prev, cur = (cur, 2.0 * cur - prev + accel)
    older = jnp.zeros_like(cur)
    adjoint = inject_local(jnp.zeros_like(cur), listing, record[0], level)
    partial_value = adjoint * accels[STEPS - 1]
    for step in range(1, STEPS):
        newer = 2.0 * adjoint - older + c2v * laplace(adjoint)
        newer = inject_local(newer, listing, record[step], level)
        partial_value = partial_value + newer * accels[STEPS - 1 - step]
        older, adjoint = (adjoint, newer)
    partial_value = partial_value * 2.0 / speed
    count = rows_own * lax.axis_size("shots")
    rows = jnp.arange(count, dtype=jnp.int32)
    wanted = own_x + jnp.arange(span_x, dtype=jnp.int32)
    select = (rows[:, None] == wanted[None, :]).astype(jnp.float32)
    placed = jnp.einsum("jx,zxy->jzy", select, partial_value, precision=highest)
    blank = jnp.zeros((count, slab_depth, width_y), jnp.float32)
    summed = lax.psum_scatter(
        lax.dynamic_update_slice_in_dim(blank, placed, own_y, 2),
        "shots",
        scatter_dimension=0,
        tiled=True,
    )
    collected = jnp.transpose(summed, (1, 0, 2))
    scaling = (model - lower_bound) * (upper_bound - model) / (upper_bound - lower_bound)
    barrier = barrier_weight / (upper_bound - model) - barrier_weight / (model - lower_bound)
    return scaling * (collected + barrier)


def solution(mesh):
    placed = (
        P("depth", "shots", None),
        P(),
        P(),
        P("shots", "depth", None, None),
        P("shots", "depth", None, None),
        P("shots", None),
        P("shots"),
        P("shots", None),
        P("shots", None, None),
    )
    return jax.shard_map(
        on_device, mesh=mesh, in_specs=placed, out_specs=P("depth", "shots", None), check_vma=False
    )
```

profile of v0, /device:TPU:4, one launch (start us, length us, event | category | flops | bytes accessed | tf_op | source)
XLA Modules:
  0.0 399.1 jit_solution(17273998616473187383)
XLA Ops:
  7.3 0.8 fusion.155
  8.1 1.1 fusion.162
  9.2 0.8 compare_select_fusion
  9.9 25.6 %scatter_custom_fusion = f32[65536]{0:T(1024)S(1)} fusion(s32[4096]{0:T(1024)S(1)} %bitcast.80, f32[4096]{0:T(1024)S(1)} %get-tuple-element.66, f32[]{:T(128)} %constant.108.clone.1), kind=kCustom, calls=%fused_computation.302 | custom fusion | flops 4096 | bytes 262148 | tf_op jit(solution)/shard_map/scatter-add | solution.py:51
  35.6 3.4 collective-permute-start.9
  39.0 3.3 collective-permute-start.8
  42.3 2.6 collective-permute-start
  45.0 3.2 collective-permute-start.1
  48.2 1.3 dynamic_slice.9
  49.5 1.4 fusion.163
  52.2 1.3 dynamic_slice.10
  55.9 1.0 collective-permute-done.9
  56.9 0.8 constant_dynamic-update-slice_fusion.3
  58.9 4.2 %collective-permute-done = f32[4,64,256]{2,1,0:T(8,128)S(1)} collective-permute-done((f32[4,64,256]{2,1,0:T(8,128)}, f32[4,64,256]{2,1,0:T(8,128)S(1)}, u32[]{:S(2)}, u32[]{:S(2)}) %collective-permute-start) | collective-permute-done | bytes 262176 | tf_op jit(solution)/shard_map/ppermute | solution.py:24
  63.1 1.5 select_maximum_fusion.12
  64.6 36.4 %all-gather.2.cloned.1.call-done = f32[4,512,512]{2,1,0:T(8,128)} async-done(((f32[4,16,512]{2,1,0:T(8,128)}), f32[4,512,512]{2,1,0:T(8,128)}) %all-gather.2.cloned.1.call-update) | async-done | bytes 4194320 | tf_op jit(solution)/shard_map/all_gather | solution.py:64
  101.0 5.0 %fusion.115 = (f32[4,64,256]{2,1,0:T(8,128)}, f32[4,64,256]{2,1,0:T(8,128)S(1)}) fusion(f32[12,72,264]{2,1,0:T(8,128)S(1)} %select_maximum_fusion.4, f32[8,64,256]{2,1,0:T(8,128)} %get-tuple-element.58, f32[8,64,256]{2,1,0:T(8,128)} %copy-done.9, f32[4,64,256]{2,1,0:T(8,128)} %copy-done.3, f32[4,64,256]{2,1,0:T(8,128)} %copy-done.2, ...), kind=kOutput, calls=%fused_computation.206 | convolution fusion | flops 404914176 | bytes 9175300 | tf_op jit(solution)/shard_map/xj,zjy->zxy/dot_general | solution.py:69
  106.0 2.3 fusion.81
  108.5 2.7 fusion.156
  111.3 2.9 collective-permute-start.3
  114.3 3.8 collective-permute-start.2
  118.2 25.8 %scatter_fusion = f32[65536]{0:T(1024)S(1)} fusion(f32[65536]{0:T(1024)S(1)} %bitcast.64, s32[4096]{0:T(1024)S(1)} %bitcast.81, f32[4096]{0:T(1024)S(1)} %get-tuple-element.65), kind=kCustom, calls=%fused_computation.1 | custom fusion | flops 4096 | bytes 65536 | tf_op jit(solution)/shard_map/scatter-add | solution.py:51
  144.1 2.0 collective-permute-start.11
  146.1 4.8 %collective-permute-start.10 = (f32[4,64,256]{2,1,0:T(8,128)S(1)}, f32[4,64,256]{2,1,0:T(8,128)S(1)}, u32[]{:S(2)}, u32[]{:S(2)}) collective-permute-start(f32[4,64,256]{2,1,0:T(8,128)S(1)} %reshape.206), channel_id=1, source_target_pairs={{1,0},{2,1},{3,2},{4,3},{5,4},{6,5},{7,6},{9,8},{10,9},{11,10},{12... | collective-permute-start | bytes 786440 | tf_op jit(solution)/shard_map/ppermute | solution.py:24
  151.3 1.1 fusion.60
  152.6 2.8 fusion.157
  155.5 1.9 collective-permute-start.5
  157.4 5.0 %collective-permute-start.4 = (f32[4,64,256]{2,1,0:T(8,128)S(1)}, f32[4,64,256]{2,1,0:T(8,128)S(1)}, u32[]{:S(2)}, u32[]{:S(2)}) collective-permute-start(f32[4,64,256]{2,1,0:T(8,128)S(1)} %subtract_add_fusion.1), channel_id=1, source_target_pairs={{1,0},{2,1},{3,2},{4,3},{5,4},{6,5},{7,6},{9,8},{10,9},{11,10},{12... | collective-permute-start | bytes 786440 | tf_op jit(solution)/shard_map/ppermute | solution.py:24
  162.5 3.5 collective-permute-done.10
  166.4 1.1 fusion.105
  167.7 25.8 %scatter_fusion.1 = f32[65536]{0:T(1024)S(1)} fusion(f32[65536]{0:T(1024)S(1)} %bitcast.65, s32[4096]{0:T(1024)S(1)} %bitcast.82, f32[4096]{0:T(1024)S(1)} %get-tuple-element.64), kind=kCustom, calls=%fused_computation.2 | custom fusion | flops 4096 | bytes 65536 | tf_op jit(solution)/shard_map/scatter-add | solution.py:51
  193.6 1.9 collective-permute-start.13
  195.5 4.8 %collective-permute-start.12 = (f32[4,64,256]{2,1,0:T(8,128)S(1)}, f32[4,64,256]{2,1,0:T(8,128)S(1)}, u32[]{:S(2)}, u32[]{:S(2)}) collective-permute-start(f32[4,64,256]{2,1,0:T(8,128)S(1)} %reshape.208), channel_id=1, source_target_pairs={{1,0},{2,1},{3,2},{4,3},{5,4},{6,5},{7,6},{9,8},{10,9},{11,10},{12... | collective-permute-start | bytes 786440 | tf_op jit(solution)/shard_map/ppermute | solution.py:24
  200.8 1.1 fusion.39
  202.0 2.7 fusion.158
  204.9 1.9 collective-permute-start.7
  206.8 4.8 %collective-permute-start.6 = (f32[4,64,256]{2,1,0:T(8,128)S(1)}, f32[4,64,256]{2,1,0:T(8,128)}, u32[]{:S(2)}, u32[]{:S(2)}) collective-permute-start(f32[4,64,256]{2,1,0:T(8,128)S(1)} %subtract_add_fusion), channel_id=1, source_target_pairs={{1,0},{2,1},{3,2},{4,3},{5,4},{6,5},{7,6},{9,8},{10,9},{11,10},{12... | collective-permute-start | bytes 786440 | tf_op jit(solution)/shard_map/ppermute | solution.py:24
  211.8 3.9 collective-permute-done.12
  216.1 1.1 fusion.95
  217.4 25.8 %scatter_fusion.2 = f32[65536]{0:T(1024)S(1)} fusion(f32[65536]{0:T(1024)S(1)} %bitcast.63, s32[4096]{0:T(1024)S(1)} %bitcast.83, f32[4096]{0:T(1024)S(1)} %get-tuple-element.63), kind=kCustom, calls=%fused_computation.3 | custom fusion | flops 4096 | bytes 65536 | tf_op jit(solution)/shard_map/scatter-add | solution.py:51
  243.3 1.4 select_maximum_fusion.6
  244.7 2.3 fusion.18
  247.1 2.7 fusion.159
  249.9 2.5 fusion.135
  252.4 2.5 broadcast_in_dim.41
  254.9 11.7 %dynamic_update_slice.3 = f32[512,4,512]{2,0,1:T(8,128)} dynamic-update-slice(f32[512,4,512]{2,0,1:T(8,128)} %broadcast_in_dim.41, f32[512,4,256]{2,0,1:T(8,128)S(1)} %copy-done, s32[]{:T(128)} %constant.111.clone.1, s32[]{:T(128)} %constant.111.clone.1, s32[]{:T(128)S(6)} %select_n.82) | dynamic-update-slice | bytes 4194308 | tf_op jit(solution)/shard_map/dynamic_update_slice | solution.py:96
  266.6 124.1 %reduce-scatter.2.cloned.1.call-done = f32[16,4,512]{2,0,1:T(8,128)} async-done(((f32[512,4,512]{2,0,1:T(8,128)}), f32[16,4,512]{2,0,1:T(8,128)}) %reduce-scatter.2.cloned.1.call-update) | async-done | bytes 131088 | tf_op jit(solution)/shard_map/reduce_scatter | solution.py:95
  390.7 1.6 fusion.145
  (68 shorter events, 6.7 us)
Async XLA Ops:
  6.5 94.5 %all-gather.2.cloned.1.call-start = ((), (), s32[]{:S(2)}) async-start(), calls=%async_computation.1 | async-start | bytes 4325376 | tf_op jit(solution)/shard_map/all_gather | solution.py:64
  7.3 383.4 %reduce-scatter.2.cloned.1.call-start = ((), (), s32[]{:S(2)}) async-start(), calls=%async_computation.2 | async-start | bytes 4325376 | tf_op jit(solution)/shard_map/reduce_scatter | solution.py:95
  35.6 21.3 %collective-permute-start.9 = (f32[4,64,256]{2,1,0:T(8,128)S(1)}, f32[4,64,256]{2,1,0:T(8,128)S(1)}, u32[]{:S(2)}, u32[]{:S(2)}) collective-permute-start(f32[4,64,256]{2,1,0:T(8,128)S(1)} %reshape.195), channel_id=1, source_target_pairs={{0,1},{1,2},{2,3},{3,4},{4,5},{5,6},{6,7},{8,9},{9,10},{10,11},{11... | collective-permute-start | bytes 786440 | tf_op jit(solution)/shard_map/ppermute | solution.py:23
  39.0 19.4 %collective-permute-start.8 = (f32[4,64,256]{2,1,0:T(8,128)S(1)}, f32[4,64,256]{2,1,0:T(8,128)S(1)}, u32[]{:S(2)}, u32[]{:S(2)}) collective-permute-start(f32[4,64,256]{2,1,0:T(8,128)S(1)} %reshape.195), channel_id=1, source_target_pairs={{1,0},{2,1},{3,2},{4,3},{5,4},{6,5},{7,6},{9,8},{10,9},{11,10},{12... | collective-permute-start | bytes 786440 | tf_op jit(solution)/shard_map/ppermute | solution.py:24
  42.3 20.7 %collective-permute-start = (f32[4,64,256]{2,1,0:T(8,128)}, f32[4,64,256]{2,1,0:T(8,128)S(1)}, u32[]{:S(2)}, u32[]{:S(2)}) collective-permute-start(f32[4,64,256]{2,1,0:T(8,128)} %bitcast.66), channel_id=1, source_target_pairs={{1,0},{2,1},{3,2},{4,3},{5,4},{6,5},{7,6},{9,8},{10,9},{11,10},{12... | collective-permute-start | bytes 786440 | tf_op jit(solution)/shard_map/ppermute | solution.py:24
  45.0 18.1 %collective-permute-start.1 = (f32[4,64,256]{2,1,0:T(8,128)}, f32[4,64,256]{2,1,0:T(8,128)}, u32[]{:S(2)}, u32[]{:S(2)}) collective-permute-start(f32[4,64,256]{2,1,0:T(8,128)} %bitcast.67), channel_id=1, source_target_pairs={{0,1},{1,2},{2,3},{3,4},{4,5},{5,6},{6,7},{8,9},{9,10},{10,11},{11... | collective-permute-start | bytes 786440 | tf_op jit(solution)/shard_map/ppermute | solution.py:23
  56.9 6.2 %copy-start.2 = (f32[4,64,256]{2,1,0:T(8,128)}, f32[4,64,256]{2,1,0:T(8,128)S(1)}, u32[]{:S(2)}) copy-start(f32[4,64,256]{2,1,0:T(8,128)S(1)} %collective-permute-done.9) | copy-start | bytes 786436
  58.4 4.7 %copy-start.1 = (f32[1,4,64,256]{3,2,1,0:T(8,128)S(1)}, f32[1,4,64,256]{3,2,1,0:T(8,128)}, u32[]{:S(2)}) copy-start(f32[1,4,64,256]{3,2,1,0:T(8,128)} %param.21) | copy-start | bytes 786436
  58.4 4.7 %copy-start.3 = (f32[4,64,256]{2,1,0:T(8,128)}, f32[4,64,256]{2,1,0:T(8,128)S(1)}, u32[]{:S(2)}) copy-start(f32[4,64,256]{2,1,0:T(8,128)S(1)} %collective-permute-done.8) | copy-start | bytes 786436
  58.5 4.6 %copy-start.9 = (f32[8,64,256]{2,1,0:T(8,128)}, f32[8,64,256]{2,1,0:T(8,128)S(1)}, u32[]{:S(2)}) copy-start(f32[8,64,256]{2,1,0:T(8,128)S(1)} %constant_dynamic-update-slice_fusion) | copy-start | bytes 1572868
  63.1 37.9 %copy-start.4 = (f32[4,64,256]{2,1,0:T(8,128)}, f32[4,64,256]{2,1,0:T(8,128)S(1)}, u32[]{:S(2)}) copy-start(f32[4,64,256]{2,1,0:T(8,128)S(1)} %collective-permute-done) | copy-start | bytes 786436
  101.0 5.0 %copy-start.5 = (f32[4,64,256]{2,1,0:T(8,128)S(1)}, f32[4,64,256]{2,1,0:T(8,128)}, u32[]{:S(2)}) copy-start(f32[4,64,256]{2,1,0:T(8,128)} %copy-done.4) | copy-start | bytes 786436
  106.0 5.2 %copy-start.8 = (f32[1,4,64,256]{3,2,1,0:T(8,128)S(1)}, f32[1,4,64,256]{3,2,1,0:T(8,128)}, u32[]{:S(2)}) copy-start(f32[1,4,64,256]{3,2,1,0:T(8,128)} %param.20) | copy-start | bytes 786436
  108.3 9.8 %copy-start.7 = (f32[4,64,256]{2,1,0:T(8,128)S(1)}, f32[4,64,256]{2,1,0:T(8,128)}, u32[]{:S(2)}) copy-start(f32[4,64,256]{2,1,0:T(8,128)} %get-tuple-element.71) | copy-start | bytes 786436
  111.3 39.6 %collective-permute-start.3 = (f32[4,64,256]{2,1,0:T(8,128)S(1)}, f32[4,64,256]{2,1,0:T(8,128)S(1)}, u32[]{:S(2)}, u32[]{:S(2)}) collective-permute-start(f32[4,64,256]{2,1,0:T(8,128)S(1)} %fusion.134), channel_id=1, source_target_pairs={{0,1},{1,2},{2,3},{3,4},{4,5},{5,6},{6,7},{8,9},{9,10},{10,11},{11... | collective-permute-start | bytes 786440 | tf_op jit(solution)/shard_map/ppermute | solution.py:23
  114.3 36.6 %collective-permute-start.2 = (f32[4,64,256]{2,1,0:T(8,128)S(1)}, f32[4,64,256]{2,1,0:T(8,128)S(1)}, u32[]{:S(2)}, u32[]{:S(2)}) collective-permute-start(f32[4,64,256]{2,1,0:T(8,128)S(1)} %fusion.134), channel_id=1, source_target_pairs={{1,0},{2,1},{3,2},{4,3},{5,4},{6,5},{7,6},{9,8},{10,9},{11,10},{12... | collective-permute-start | bytes 786440 | tf_op jit(solution)/shard_map/ppermute | solution.py:24
  144.1 18.3 %collective-permute-start.11 = (f32[4,64,256]{2,1,0:T(8,128)S(1)}, f32[4,64,256]{2,1,0:T(8,128)S(1)}, u32[]{:S(2)}, u32[]{:S(2)}) collective-permute-start(f32[4,64,256]{2,1,0:T(8,128)S(1)} %reshape.206), channel_id=1, source_target_pairs={{0,1},{1,2},{2,3},{3,4},{4,5},{5,6},{6,7},{8,9},{9,10},{10,11},{11... | collective-permute-start | bytes 786440 | tf_op jit(solution)/shard_map/ppermute | solution.py:23
  146.1 19.9 %collective-permute-start.10 = (f32[4,64,256]{2,1,0:T(8,128)S(1)}, f32[4,64,256]{2,1,0:T(8,128)S(1)}, u32[]{:S(2)}, u32[]{:S(2)}) collective-permute-start(f32[4,64,256]{2,1,0:T(8,128)S(1)} %reshape.206), channel_id=1, source_target_pairs={{1,0},{2,1},{3,2},{4,3},{5,4},{6,5},{7,6},{9,8},{10,9},{11,10},{12... | collective-permute-start | bytes 786440 | tf_op jit(solution)/shard_map/ppermute | solution.py:24
  155.5 44.8 %collective-permute-start.5 = (f32[4,64,256]{2,1,0:T(8,128)S(1)}, f32[4,64,256]{2,1,0:T(8,128)S(1)}, u32[]{:S(2)}, u32[]{:S(2)}) collective-permute-start(f32[4,64,256]{2,1,0:T(8,128)S(1)} %subtract_add_fusion.1), channel_id=1, source_target_pairs={{0,1},{1,2},{2,3},{3,4},{4,5},{5,6},{6,7},{8,9},{9,10},{10,11},{11... | collective-permute-start | bytes 786440 | tf_op jit(solution)/shard_map/ppermute | solution.py:23
  157.4 42.9 %collective-permute-start.4 = (f32[4,64,256]{2,1,0:T(8,128)S(1)}, f32[4,64,256]{2,1,0:T(8,128)S(1)}, u32[]{:S(2)}, u32[]{:S(2)}) collective-permute-start(f32[4,64,256]{2,1,0:T(8,128)S(1)} %subtract_add_fusion.1), channel_id=1, source_target_pairs={{1,0},{2,1},{3,2},{4,3},{5,4},{6,5},{7,6},{9,8},{10,9},{11,10},{12... | collective-permute-start | bytes 786440 | tf_op jit(solution)/shard_map/ppermute | solution.py:24
  193.6 18.1 %collective-permute-start.13 = (f32[4,64,256]{2,1,0:T(8,128)S(1)}, f32[4,64,256]{2,1,0:T(8,128)S(1)}, u32[]{:S(2)}, u32[]{:S(2)}) collective-permute-start(f32[4,64,256]{2,1,0:T(8,128)S(1)} %reshape.208), channel_id=1, source_target_pairs={{0,1},{1,2},{2,3},{3,4},{4,5},{5,6},{6,7},{8,9},{9,10},{10,11},{11... | collective-permute-start | bytes 786440 | tf_op jit(solution)/shard_map/ppermute | solution.py:23
  195.5 20.2 %collective-permute-start.12 = (f32[4,64,256]{2,1,0:T(8,128)S(1)}, f32[4,64,256]{2,1,0:T(8,128)S(1)}, u32[]{:S(2)}, u32[]{:S(2)}) collective-permute-start(f32[4,64,256]{2,1,0:T(8,128)S(1)} %reshape.208), channel_id=1, source_target_pairs={{1,0},{2,1},{3,2},{4,3},{5,4},{6,5},{7,6},{9,8},{10,9},{11,10},{12... | collective-permute-start | bytes 786440 | tf_op jit(solution)/shard_map/ppermute | solution.py:24
  204.9 38.4 %collective-permute-start.7 = (f32[4,64,256]{2,1,0:T(8,128)S(1)}, f32[4,64,256]{2,1,0:T(8,128)S(1)}, u32[]{:S(2)}, u32[]{:S(2)}) collective-permute-start(f32[4,64,256]{2,1,0:T(8,128)S(1)} %subtract_add_fusion), channel_id=1, source_target_pairs={{0,1},{1,2},{2,3},{3,4},{4,5},{5,6},{6,7},{8,9},{9,10},{10,11},{11... | collective-permute-start | bytes 786440 | tf_op jit(solution)/shard_map/ppermute | solution.py:23
  206.8 36.4 %collective-permute-start.6 = (f32[4,64,256]{2,1,0:T(8,128)S(1)}, f32[4,64,256]{2,1,0:T(8,128)}, u32[]{:S(2)}, u32[]{:S(2)}) collective-permute-start(f32[4,64,256]{2,1,0:T(8,128)S(1)} %subtract_add_fusion), channel_id=1, source_target_pairs={{1,0},{2,1},{3,2},{4,3},{5,4},{6,5},{7,6},{9,8},{10,9},{11,10},{12... | collective-permute-start | bytes 786440 | tf_op jit(solution)/shard_map/ppermute | solution.py:24
  252.4 2.5 copy-start
  266.6 124.1 %copy-start.6 = (f32[4,16,512]{2,1,0:T(8,128)S(1)}, f32[4,16,512]{2,1,0:T(8,128)}, u32[]{:S(2)}) copy-start(f32[4,16,512]{2,1,0:T(8,128)} %param.17) | copy-start | bytes 393220
Sparse Core Ops, SparseCore 0:
  10.2 90.7 all-gather.1
  266.7 123.8 reduce-scatter.1
where the time goes:
time: 400 us; the launch traced here: 399 us
  waiting for transfers between devices  174 us (44%)
  other arithmetic  132 us (33%)
  starting transfers between devices  46.5 us (12%)
  local copies, waits for them, and re-layouts  22.5 us (6%)
  between operations  16.5 us (4%)
  matrix products  7.49 us (2%)
    reduce_scatter x1, waiting for transfers between devices, on_device(): lax.psum_scatter(lax.dynamic_update_slice_in_dim(blank, placed, own_y, 2)...  124 us
    scatter-add x8, other arithmetic, inject_local(): field.reshape(-1).at[local_places].add(local_values).reshape(field.shape)  114 us
    all_gather x1, waiting for transfers between devices, on_device(): piece = lax.all_gather(model, 'shots', axis=1, tiled=True)  36.4 us
    ppermute x7, starting transfers between devices, padded_2(): after = lax.ppermute(first, axis, down)  29.1 us
    ppermute x7, starting transfers between devices, padded_2(): before = lax.ppermute(last, axis, up)  17.3 us
    dynamic_update_slice x1, local copies, waits for them, and re-layouts, on_device(): lax.dynamic_update_slice_in_dim(blank, placed, own_y, 2)  11.7 us
    ppermute x7, waiting for transfers between devices, padded_2(): after = lax.ppermute(first, axis, down)  11.6 us
  transfers between devices with their start and end apart: 16, of which 6 were waited for; matrix products, arithmetic and copies ran while one was open for 32% of the time, Pallas kernels for 0%

commit v1 on v0

v1 whole, which is shorter than its diff:
```python
import functools

import jax
import jax.numpy as jnp
from jax import lax
from jax.experimental import pallas as pl
from jax.experimental.pallas import tpu as pltpu
from jax.sharding import PartitionSpec as P

MESH = pl.DeviceIdType.MESH
F32 = jnp.float32
BF16 = jnp.bfloat16
STEPS = 4

stencil_weights = (-205.0 / 72.0, 8.0 / 5.0, -1.0 / 5.0, 8.0 / 315.0, -1.0 / 560.0)
courant = 0.095
lower_bound = 1.0
upper_bound = 5.0
barrier_weight = 0.5

PARTS = 8
LOCAL = 4
PLANES = 16
SPAN = 64
LANES = 128
ROWS = 16
HALO = 16
OWN = 32
CHUNK = 512
PAD = 8


def iota(shape, dim):
    return lax.broadcasted_iota(jnp.int32, shape, dim)


def window(first, second, part):
    rows = first[0].shape[0]
    lane = iota((rows, LANES), 1)
    zero = jnp.zeros((rows, LANES), F32)
    start = OWN * part - HALO
    tile, at = start // LANES, start % LANES

    def pick(tiles, k):
        return tiles[k] if 0 <= k < 2 else zero

    half = lane - at if at <= 64 else lane - at + LANES
    if at <= 64:
        low = pick(first, tile)
        in_low = (lane >= at) & (lane < at + 64)
        own = (lane + 64) % LANES
        high = jnp.where(own >= at, pick(second, tile), pick(second, tile + 1))
        if at == 0:
            high = pick(second, tile)
    else:
        low = jnp.where(lane >= at, pick(first, tile), pick(first, tile + 1))
        in_low = (lane >= at) | (lane < at - 64)
        own = (lane + 64) % LANES
        high = jnp.where(own >= at, pick(second, tile), pick(second, tile + 1))
    del half
    both = jnp.where(in_low, low, high)
    return pltpu.roll(both, (LANES - at) % LANES, 1) if at else both


def kernel(
    near,
    offx, offy, pulse, place, model, prev, cur, listing, record,
    out,
    gathered, stage, fields, lams, shifted, onto, summed_r, windows, arrived, speeds, c2v, first_lap, accels, partial,
    packed, outgoing, landed, placed, totals, ring_p, ring_m,
    gp_send, gp_recv, gm_send, gm_recv, ck_send, ck_recv, w_send, w_recv, o_send, o_recv,
    rp_send, rp_recv, rm_send, rm_recv,
):
    shot = lax.axis_index("shots")
    part = lax.axis_index("depth")
    level = lax.div(shot, LOCAL)
    group = lax.rem(shot, LOCAL)
    me = group * PARTS + part
    peers = LOCAL * PARTS
    up = lax.rem(level + 1, near)
    down = lax.rem(level + near - 1, near)
    lane = iota((SPAN, LANES), 1)
    lower = lane < 64

    def device(k):
        return (LOCAL * level + lax.div(k, PARTS), lax.rem(k, PARTS))

    barrier = pltpu.get_barrier_semaphore()

    def greet(k, carry):
        pl.semaphore_signal(barrier, inc=1, device_id=device(lax.rem(me + k, peers)), device_id_type=MESH)
        return carry

    for other in (up, down):
        pl.semaphore_signal(barrier, inc=1, device_id=(LOCAL * other + group, part), device_id_type=MESH)
    lax.fori_loop(1, peers, greet, 0)

    for tile in range(4):
        gathered[level, :, tile] = model[:, :, pl.ds(LANES * tile, LANES)]
    for which, source in ((0, cur), (1, prev)):
        for i in range(2):
            low = [source[0, i, :, pl.ds(LANES * k, LANES)] for k in range(2)]
            high = [pltpu.roll(source[0, 2 + i, :, pl.ds(LANES * k, LANES)], 64, 1) for k in range(2)]
            for to in range(PARTS):
                stage[which, to, i] = window(low, high, to)

    pl.semaphore_wait(barrier, peers + 1)

    def ring_copy(m, sign, send, recv):
        origin = lax.rem(level + near - sign * lax.div(m, 2) + near, near)
        chunk = lax.rem(m, 2) if sign > 0 else 1 - lax.rem(m, 2)
        where = gathered.at[origin, pl.ds(2 * chunk, 2)]
        to = up if sign > 0 else down
        return pltpu.make_async_remote_copy(
            src_ref=where, dst_ref=where, send_sem=send.at[m], recv_sem=recv.at[m],
            device_id=(LOCAL * to + group, part), device_id_type=MESH,
        )

    def ring_wait(m, sign, send, recv):
        origin = lax.rem(level + near - sign * (lax.div(m, 2) + 1) + near, near)
        chunk = lax.rem(m, 2) if sign > 0 else 1 - lax.rem(m, 2)
        where = gathered.at[origin, pl.ds(2 * chunk, 2)]
        to = up if sign > 0 else down
        pltpu.make_async_remote_copy(
            src_ref=where, dst_ref=where, send_sem=send.at[m], recv_sem=recv.at[m],
            device_id=(LOCAL * to + group, part), device_id_type=MESH,
        ).wait_recv()

    def ckpt_copy(which, to, origin):
        return pltpu.make_async_remote_copy(
            src_ref=stage.at[which, to],
            dst_ref=fields.at[which, pl.ds(2 + 2 * origin, 2), pl.ds(PAD, SPAN)],
            send_sem=ck_send.at[which, to], recv_sem=ck_recv.at[which, origin],
            device_id=(shot, to), device_id_type=MESH,
        )

    ring_copy(0, 1, gp_send, gp_recv).start()
    ring_copy(0, -1, gm_send, gm_recv).start()
    ring_copy(1, 1, gp_send, gp_recv).start()
    ring_copy(1, -1, gm_send, gm_recv).start()

    def ckpt_start(k, carry):
        to = lax.rem(part + k, PARTS)
        ckpt_copy(0, to, part).start()
        ckpt_copy(1, to, part).start()
        return carry

    lax.fori_loop(1, PARTS, ckpt_start, 0)

    for ref, slots in ((fields, 2), (lams, 3)):
        for slot in range(slots):
            for edge in (0, 1, PLANES + 2, PLANES + 3):
                ref[slot, edge] = jnp.zeros((SPAN + 2 * PAD, LANES), F32)
            for edge in range(2, PLANES + 2):
                ref[slot, edge, pl.ds(0, PAD)] = jnp.zeros((PAD, LANES), F32)
                ref[slot, edge, pl.ds(PAD + SPAN, PAD)] = jnp.zeros((PAD, LANES), F32)
    for which in range(2):
        fields[which, pl.ds(2 + 2 * part, 2), pl.ds(PAD, SPAN)] = stage[which, part]
    for b in range(LOCAL):
        for tile in (0, 1, 5):
            placed[b, :, tile] = jnp.zeros((4, ROWS, LANES), F32)

    summed_r[...] = jnp.zeros(summed_r.shape, F32)

    def receivers(step):
        at = pl.ds(pl.multiple_of(step * CHUNK, CHUNK), CHUNK)
        flat = listing[:, at]
        zc = lax.shift_right_logical(flat, 14)
        x = lax.shift_right_logical(flat, 8) & 63
        y = (flat & 255) - (OWN * part - HALO)
        row = (lax.shift_right_logical(zc, 2) * 2 + (zc & 1)) * SPAN + x
        column = jnp.where((y >= 0) & (y < 64), (lax.shift_right_logical(zc, 1) & 1) * 64 + y, -1)
        hot = (iota((PLANES * SPAN, CHUNK), 0) == row).astype(F32).astype(BF16)
        match = iota((LANES, CHUNK), 0) == column
        for k in range(STEPS):
            value = record[0, pl.ds(k, 1), at]
            high = value.astype(BF16).astype(F32)
            rest = value - high
            onto[pl.ds(LANES * k, LANES), pl.ds(0, CHUNK)] = jnp.where(match, high, 0.0).astype(BF16)
            onto[pl.ds(LANES * k, LANES), pl.ds(CHUNK, CHUNK)] = jnp.where(match, rest, 0.0).astype(BF16)
        dims = (((1,), (1,)), ((), ()))
        total = lax.dot_general(hot, onto[:, pl.ds(0, CHUNK)], dims, preferred_element_type=F32)
        total = total + lax.dot_general(hot, onto[:, pl.ds(CHUNK, CHUNK)], dims, preferred_element_type=F32)
        summed_r[...] += total

    def ring_step(m, carry):
        ring_wait(m - 2, 1, gp_send, gp_recv)
        ring_copy(m, 1, gp_send, gp_recv).start()
        ring_wait(m - 2, -1, gm_send, gm_recv)
        ring_copy(m, -1, gm_send, gm_recv).start()
        receivers(m)
        return carry

    def two_first(m, carry):
        receivers(m)
        return carry

    lax.fori_loop(0, 2, two_first, 0)
    lax.fori_loop(2, 7, ring_step, 0)
    receivers(7)

    def laplace(field, slot, e):
        result = []
        at = 2 + 2 * e

        def own(k):
            return field[slot, at + k, pl.ds(PAD, SPAN)]

        def other(k):
            return shifted[at + k]

        along_z = (
            ((own(1), other(-1)), (other(0), other(-2)), (other(1), own(-1)), (own(2), own(-2))),
            ((other(0), own(0)), (other(1), other(-1)), (own(2), other(-2)), (own(3), own(-1))),
        )
        for i in range(2):
            middle = own(i)
            total = 3.0 * stencil_weights[0] * middle
            for k in range(1, 5):
                some = along_z[i][k - 1][0] + along_z[i][k - 1][1]
                some = some + field[slot, at + i, pl.ds(PAD + k, SPAN)]
                some = some + field[slot, at + i, pl.ds(PAD - k, SPAN)]
                some = some + pltpu.roll(middle, k, 1)
                some = some + pltpu.roll(middle, LANES - k, 1)
                total = total + stencil_weights[k] * some
            result.append(total)
        return result

    def shift(field, slot):
        def one(p, carry):
            both = jnp.where(lower, field[slot, p + 2, pl.ds(PAD, SPAN)], field[slot, p, pl.ds(PAD, SPAN)])
            shifted[p] = pltpu.roll(both, 64, 1)
            return carry

        lax.fori_loop(0, PLANES + 2, one, 0)

    def residual(k, p):
        return summed_r[pl.ds(pl.multiple_of(p * SPAN, SPAN), SPAN), pl.ds(LANES * k, LANES)]

    def to_lam(p, carry):
        lams[0, p + 2, pl.ds(PAD, SPAN)] = residual(0, p)
        return carry

    lax.fori_loop(0, PLANES, to_lam, 0)

    def ckpt_wait(k, carry):
        origin = lax.rem(part + k, PARTS)
        ckpt_copy(0, part, origin).wait_recv()
        ckpt_copy(1, part, origin).wait_recv()
        return carry

    lax.fori_loop(1, PARTS, ckpt_wait, 0)

    def keep_lap(field, slot, which):
        shift(field, slot)

        def one(e, carry):
            for i, value in enumerate(laplace(field, slot, e)):
                first_lap[which, 2 * e + i] = value
            return carry

        lax.fori_loop(0, PARTS, one, 0)

    keep_lap(fields, 0, 0)
    keep_lap(lams, 0, 1)

    for m in (5, 6):
        ring_wait(m, 1, gp_send, gp_recv)
        ring_wait(m, -1, gm_send, gm_recv)

    small = iota((ROWS, LANES), 1)
    row16 = iota((ROWS, LANES), 0)

    def window_copy(to, origin):
        return pltpu.make_async_remote_copy(
            src_ref=windows.at[to],
            dst_ref=arrived.at[pl.ds(2 * lax.rem(origin, PARTS), 2), pl.ds(ROWS * lax.div(origin, PARTS), ROWS)],
            send_sem=w_send.at[to], recv_sem=w_recv.at[origin],
            device_id=device(to), device_id_type=MESH,
        )

    def spot(b):
        ox = offx[LOCAL * level + b]
        oy = offy[LOCAL * level + b]
        t = ox - ROWS * group + SPAN
        return lax.shift_right_logical(t, 6) - 1, t & 63, lax.shift_right_logical(oy, 7), oy & 127

    def cut(b, carry):
        block, rest, tile, at = spot(b)
        upper_rows = row16 >= rest
        q0 = jnp.maximum(block, 0)
        q1 = jnp.minimum(block + 1, near - 1)
        back = lax.rem(LANES - at, LANES)
        keep = small < LANES - at
        planes = []
        for plane in range(4):
            turned_tiles = []
            for k in range(3):
                t = jnp.minimum(tile + k, 3)
                mixed = jnp.where(upper_rows, gathered[q0, plane, t], gathered[q1, plane, t])
                turned_tiles.append(pltpu.roll(mixed, back, 1))
            planes.append([jnp.where(keep, turned_tiles[k], turned_tiles[k + 1]) for k in range(2)])
        for i in range(2):
            high = [pltpu.roll(v, 64, 1) for v in planes[2 + i]]
            for to in range(PARTS):
                windows[b * PARTS + to, i] = window(planes[i], high, to)
        for to in range(PARTS):
            @pl.when(b * PARTS + to != me)
            def _():
                window_copy(b * PARTS + to, me).start()
        return carry

    lax.fori_loop(0, LOCAL, cut, 0)
    arrived[pl.ds(2 * part, 2), pl.ds(ROWS * group, ROWS)] = windows[me]

    def window_wait(k, carry):
        window_copy(me, lax.rem(me + k, peers)).wait_recv()
        return carry

    lax.fori_loop(1, peers, window_wait, 0)

    turn = offx[shot] & 63

    def make_c2v(p, carry):
        arrived[p, pl.ds(SPAN, SPAN)] = arrived[p, pl.ds(0, SPAN)]
        speed = arrived[p, pl.ds(turn, SPAN)]
        speeds[p] = speed
        scaled = courant * speed
        c2v[p] = scaled * scaled
        return carry

    lax.fori_loop(0, PLANES, make_c2v, 0)

    flat = place[0]
    zc = lax.shift_right_logical(flat, 14)
    sy = (flat & 255) - (OWN * part - HALO)
    s_plane = lax.shift_right_logical(zc, 2) * 2 + (zc & 1)
    s_lane = jnp.where((sy >= 0) & (sy < 64), (lax.shift_right_logical(zc, 1) & 1) * 64 + sy, -1)
    at_source = (lane == s_lane) & (iota((SPAN, LANES), 0) == (lax.shift_right_logical(flat, 8) & 63))

    def accel_of(value, p, n):
        strength = jnp.where(p == s_plane, pulse[0, n], 0.0)
        return c2v[p] * value + jnp.where(at_source, strength, 0.0)

    inner = pl.ds(PAD, SPAN)

    for n in range(STEPS):
        now, old = n % 2, 1 - n % 2
        if n:
            shift(fields, now)

        def forward(e, carry, n=n, now=now, old=old):
            laps = laplace(fields, now, e) if n else [first_lap[0, 2 * e + i] for i in range(2)]
            for i in range(2):
                p = 2 * e + i
                accel = accel_of(laps[i], p, n)
                accels[n, p] = accel
                if n < STEPS - 1:
                    fields[old, p + 2, inner] = (
                        2.0 * fields[now, p + 2, inner] - fields[old, p + 2, inner] + accel
                    )
            return carry

        lax.fori_loop(0, PARTS, forward, 0)

    def out_copy(to, origin):
        return pltpu.make_async_remote_copy(
            src_ref=outgoing.at[lax.rem(to, PARTS), pl.ds(ROWS * lax.div(to, PARTS), ROWS)],
            dst_ref=landed.at[origin],
            send_sem=o_send.at[to], recv_sem=o_recv.at[origin],
            device_id=device(to), device_id_type=MESH,
        )

    for k in range(1, STEPS):
        now, old, new = (k - 1) % 3, (k - 2) % 3, k % 3
        if k > 1:
            shift(lams, now)

        def adjoint(e, carry, k=k, now=now, old=old, new=new):
            laps = laplace(lams, now, e) if k > 1 else [first_lap[1, 2 * e + i] for i in range(2)]
            parts = []
            for i in range(2):
                p = 2 * e + i
                lam = lams[now, p + 2, inner]
                newer = 2.0 * lam + c2v[p] * laps[i] + residual(k, p)
                if k > 1:
                    newer = newer - lams[old, p + 2, inner]
                    so_far = partial[p]
                else:
                    so_far = lam * accels[STEPS - 1, p]
                so_far = so_far + newer * accels[STEPS - 1 - k, p]
                if k < STEPS - 1:
                    lams[new, p + 2, inner] = newer
                    partial[p] = so_far
                else:
                    parts.append(so_far * 2.0 / speeds[p])
            if k == STEPS - 1:
                both = jnp.where(
                    (lane & 63) < OWN, pltpu.roll(parts[0], LANES - HALO, 1), pltpu.roll(parts[1], OWN - HALO, 1)
                )
                packed[e, pl.ds(0, SPAN)] = both
                packed[e, pl.ds(SPAN, SPAN)] = both
                outgoing[e] = packed[e, pl.ds((SPAN - turn) & 63, SPAN)]
                for b in range(LOCAL):
                    @pl.when(b * PARTS + e != me)
                    def _():
                        out_copy(b * PARTS + e, me).start()
            return carry

        lax.fori_loop(0, PARTS, adjoint, 0)

    landed[me] = outgoing[part, pl.ds(pl.multiple_of(ROWS * group, ROWS), ROWS)]

    def out_wait(k, carry):
        out_copy(me, lax.rem(me + k, peers)).wait_recv()
        return carry

    lax.fori_loop(1, peers, out_wait, 0)

    def put(b, carry):
        block, rest, tile, at = spot(b)
        group_of = lax.shift_right_logical(small, 5)
        keep = small >= at
        for plane in range(4):
            halves = []
            for k in range(2):
                total = None
                for c in range(4):
                    piece = landed[b * PARTS + 4 * k + c]
                    by = (OWN * (c - plane)) % LANES
                    if by:
                        piece = pltpu.roll(piece, by, 1)
                    total = piece if total is None else jnp.where(group_of == c, piece, total)
                halves.append(pltpu.roll(total, at, 1))
            placed[b, plane, 2] = jnp.where(keep, halves[0], 0.0)
            placed[b, plane, 3] = jnp.where(keep, halves[1], halves[0])
            placed[b, plane, 4] = jnp.where(keep, 0.0, halves[1])
        return carry

    lax.fori_loop(0, LOCAL, put, 0)

    spots = [spot(b) for b in range(LOCAL)]
    blocks = [jnp.where(iota((4, ROWS, LANES), 1) >= s[1], s[0], s[0] + 1) for s in spots]

    def add_up(plane, carry):
        cells = [
            placed[b, plane, pl.ds(2 - spots[b][2], 4)]
            for b in range(LOCAL)
        ]

        def one(q, carry):
            total = jnp.where(blocks[0] == q, cells[0], 0.0)
            for b in range(1, LOCAL):
                total = total + jnp.where(blocks[b] == q, cells[b], 0.0)
            totals[q, plane] = total
            return carry

        return lax.fori_loop(0, near, one, carry)

    lax.fori_loop(0, 4, add_up, 0)

    half = near // 2

    def sum_chunk(m, sign):
        odd = m % 2
        return odd if sign > 0 else 1 - odd

    def sum_copy(m, sign, ring, send, recv):
        target = lax.rem(level + near + sign * (half - (m + 1) // 2), near)
        to = up if sign > 0 else down
        return pltpu.make_async_remote_copy(
            src_ref=totals.at[target, pl.ds(2 * sum_chunk(m, sign), 2)], dst_ref=ring.at[m],
            send_sem=send.at[m], recv_sem=recv.at[m],
            device_id=(LOCAL * to + group, part), device_id_type=MESH,
        )

    ways = ((1, ring_p, rp_send, rp_recv), (-1, ring_m, rm_send, rm_recv))
    for m in range(near - 1):
        for sign, ring, send, recv in ways:
            if m >= 2:
                sum_copy(m - 2, sign, ring, send, recv).wait_recv()
                target = lax.rem(level + near + sign * (half - (m + 1) // 2), near)
                where = pl.ds(2 * sum_chunk(m, sign), 2)
                totals[target, where] = totals[target, where] + ring[m - 2]
            sum_copy(m, sign, ring, send, recv).start()
    for m in (near - 3, near - 2):
        for sign, ring, send, recv in ways:
            sum_copy(m, sign, ring, send, recv).wait_recv()
    for c in range(2):
        where = pl.ds(2 * c, 2)
        total = totals[level, where]
        for sign, ring, send, recv in ways:
            for m in (near - 3, near - 2):
                if sum_chunk(m, sign) == c:
                    total = total + ring[m]
        speed = model[where]
        total = jnp.concatenate([total[:, tile] for tile in range(4)], axis=-1)
        scaling = (speed - lower_bound) * (upper_bound - speed) / (upper_bound - lower_bound)
        limit = barrier_weight / (upper_bound - speed) - barrier_weight / (speed - lower_bound)
        out[where] = scaling * (total + limit)

    for m in range(near - 1):
        ring_copy(m, 1, gp_send, gp_recv).wait_send()
        ring_copy(m, -1, gm_send, gm_recv).wait_send()
        for sign, ring, send, recv in ways:
            sum_copy(m, sign, ring, send, recv).wait_send()

    def ckpt_sent(k, carry):
        to = lax.rem(part + k, PARTS)
        ckpt_copy(0, to, part).wait_send()
        ckpt_copy(1, to, part).wait_send()
        return carry

    lax.fori_loop(1, PARTS, ckpt_sent, 0)

    def blocks_sent(k, carry):
        to = lax.rem(me + k, peers)
        window_copy(to, me).wait_send()
        out_copy(to, me).wait_send()
        return carry

    lax.fori_loop(1, peers, blocks_sent, 0)


def on_device(near, model, offsets_x, offsets_y, ckpt_prev, ckpt_cur, wavelet, source, receivers, traces):
    peers = LOCAL * PARTS
    vmem = pl.BlockSpec(memory_space=pltpu.VMEM)
    smem = pl.BlockSpec(memory_space=pltpu.SMEM)
    padded = (PLANES + 4, SPAN + 2 * PAD, LANES)
    plain = (PLANES, SPAN, LANES)
    dma = pltpu.SemaphoreType.DMA
    return pl.pallas_call(
        functools.partial(kernel, near),
        out_shape=jax.ShapeDtypeStruct(model.shape, F32),
        in_specs=[smem] * 4 + [vmem] * 5,
        out_specs=vmem,
        scratch_shapes=[
            pltpu.VMEM((near, 4, 4, ROWS, LANES), F32),
            pltpu.VMEM((2, PARTS, 2, SPAN, LANES), F32),
            pltpu.VMEM((2,) + padded, F32),
            pltpu.VMEM((3,) + padded, F32),
            pltpu.VMEM((PLANES + 2, SPAN, LANES), F32),
            pltpu.VMEM((STEPS * LANES, 2 * CHUNK), BF16),
            pltpu.VMEM((PLANES * SPAN, STEPS * LANES), F32),
            pltpu.VMEM((peers, 2, ROWS, LANES), F32),
            pltpu.VMEM((PLANES, 2 * SPAN, LANES), F32),
            pltpu.VMEM(plain, F32),
            pltpu.VMEM(plain, F32),
            pltpu.VMEM((2,) + plain, F32),
            pltpu.VMEM((STEPS,) + plain, F32),
            pltpu.VMEM(plain, F32),
            pltpu.VMEM((PARTS, 2 * SPAN, LANES), F32),
            pltpu.VMEM((PARTS, SPAN, LANES), F32),
            pltpu.VMEM((peers, ROWS, LANES), F32),
            pltpu.VMEM((LOCAL, 4, 6, ROWS, LANES), F32),
            pltpu.VMEM((near, 4, 4, ROWS, LANES), F32),
            pltpu.VMEM((near - 1, 2, 4, ROWS, LANES), F32),
            pltpu.VMEM((near - 1, 2, 4, ROWS, LANES), F32),
            dma((near - 1,)), dma((near - 1,)), dma((near - 1,)), dma((near - 1,)),
            dma((2, PARTS)), dma((2, PARTS)),
            dma((peers,)), dma((peers,)), dma((peers,)), dma((peers,)),
            dma((near - 1,)), dma((near - 1,)), dma((near - 1,)), dma((near - 1,)),
        ],
        compiler_params=pltpu.CompilerParams(
            collective_id=0, has_side_effects=True, vmem_limit_bytes=48 * 1024 * 1024
        ),
    )(offsets_x, offsets_y, wavelet, source, model, ckpt_prev, ckpt_cur, receivers, traces)


def solution(mesh):
    placed = (
        P("depth", "shots", None),
        P(),
        P(),
        P("shots", "depth", None, None),
        P("shots", "depth", None, None),
        P("shots", None),
        P("shots"),
        P("shots", None),
        P("shots", None, None),
    )
    near = mesh.shape["shots"] // LOCAL
    return jax.shard_map(
        functools.partial(on_device, near),
        mesh=mesh, in_specs=placed, out_specs=P("depth", "shots", None), check_vma=False,
    )
```

time: 400 us -> 88.8 us (0.22)
  waiting for transfers between devices: 174 us -> 0 us
  other arithmetic: 132 us -> 0 us
  Pallas kernels: 0 us -> 82.8 us
  starting transfers between devices: 46.5 us -> 0 us
  local copies, waits for them, and re-layouts: 22.5 us -> 5.02 us
  between operations: 16.5 us -> 0.74 us
  matrix products: 7.49 us -> 0 us
    reduce_scatter x1 -> x0, waiting for transfers between devices: 124 us -> none  [on_device(): lax.psum_scatter(lax.dynamic_update_slice_in_dim(blank, placed, own_y, 2)...]
    scatter-add x8 -> x0, other arithmetic: 114 us -> none  [inject_local(): field.reshape(-1).at[local_places].add(local_values).reshape(field.shape)]
    pallas_call x0 -> x1, Pallas kernels: none -> 82.8 us  [on_device(): pl.pallas_call(functools.partial(kernel, near), out_shape=jax.ShapeDtypeS...]
    ppermute x14 -> x0, starting transfers between devices: 46.5 us -> none  [the longest x7 29.1 us: padded_2(): after = lax.ppermute(first, axis, down)]
    all_gather x1 -> x0, waiting for transfers between devices: 36.4 us -> none  [on_device(): piece = lax.all_gather(model, 'shots', axis=1, tiled=True)]
    ppermute x14 -> x0, waiting for transfers between devices: 12.6 us -> none  [the longest x7 11.6 us: padded_2(): after = lax.ppermute(first, axis, down)]
    dynamic_update_slice x1 -> x0, local copies, waits for them, and re-layouts: 11.7 us -> none  [on_device(): lax.dynamic_update_slice_in_dim(blank, placed, own_y, 2)]
    mul x5 -> x0, other arithmetic: 8.36 us -> none  [the longest x4 6.75 us: on_device(): c2v * laplace(cur)]
  transfers between devices with their start and end apart: 16 -> 0, of which waited for: 6 -> 0; matrix products, arithmetic and copies ran while one was open for 32% -> 0% of each run, Pallas kernels for 0% -> 0%
where the time goes in v1:
time: 88.8 us; the launch traced here: 88.5 us
  Pallas kernels  82.8 us (93%)
  local copies, waits for them, and re-layouts  5.02 us (6%)
    pallas_call x1, Pallas kernels, on_device(): pl.pallas_call(functools.partial(kernel, near), out_shape=jax.ShapeDtypeS...  82.8 us
    unnamed x17, local copies, waits for them, and re-layouts  5.02 us

profile of v1, /device:TPU:4, one launch (start us, length us, event | category | flops | bytes accessed | tf_op | source)
XLA Modules:
  0.0 88.5 jit_solution(2180359791828145839)
XLA Ops:
  0.0 0.0 copy-start.7
  0.0 0.0 copy-start.6
  0.0 0.0 copy-start.5
  0.7 0.0 copy-done.7
  0.7 0.0 copy-done.6
  0.7 0.0 copy-done.5
  0.7 0.0 copy-start
  0.7 0.9 %copy-done = f32[1,4,64,256]{3,2,1,0:T(8,128)S(1)} copy-done((f32[1,4,64,256]{3,2,1,0:T(8,128)S(1)}, f32[1,4,64,256]{3,2,1,0:T(8,128)}, u32[]{:S(2)}) %copy-start) | copy-done | bytes 262168
  1.7 0.0 copy-start.1
  1.7 0.9 %copy-done.1 = f32[1,4,64,256]{3,2,1,0:T(8,128)S(1)} copy-done((f32[1,4,64,256]{3,2,1,0:T(8,128)S(1)}, f32[1,4,64,256]{3,2,1,0:T(8,128)}, u32[]{:S(2)}) %copy-start.1) | copy-done | bytes 262168
  2.6 0.0 copy-start.2
  2.6 0.9 %copy-done.2 = f32[4,16,512]{2,1,0:T(8,128)S(1)} copy-done((f32[4,16,512]{2,1,0:T(8,128)S(1)}, f32[4,16,512]{2,1,0:T(8,128)}, u32[]{:S(2)}) %copy-start.2) | copy-done | bytes 131096
  3.5 0.0 copy-start.3
  3.5 0.8 copy-done.3
  4.4 0.0 copy-start.4
  4.4 0.7 copy-done.4
  5.1 82.8 %shard_map.91 = f32[4,16,512]{2,1,0:T(8,128)S(1)} custom-call(s32[32]{0:T(128)S(1)} %copy-done.5, s32[32]{0:T(128)S(1)} %copy-done.6, f32[1,4]{1,0:T(1,128)S(1)} %copy-done.7, s32[1]{0:T(128)S(6)} %copy.11.place, f32[4,16,512]{2,1,0:T(8,128)S(1)} %copy-done.2, f32[1,4,64,256]{3,2,1,0:T(8,128)S(1)} %copy-done, f32[1,4,64,256]{3,2,1,0:T(8,128)S(1)} %copy-done.1, ...), custom_call_target="tpu_custom_call" | custom-call | tf_op jit(solution)/shard_map/pallas_call | solution.py:532
  87.9 0.7 copy.12
Async XLA Ops:
  0.0 0.7 copy-start.7
  0.0 0.7 copy-start.6
  0.0 0.7 copy-start.5
  0.7 1.0 %copy-start = (f32[1,4,64,256]{3,2,1,0:T(8,128)S(1)}, f32[1,4,64,256]{3,2,1,0:T(8,128)}, u32[]{:S(2)}) copy-start(f32[1,4,64,256]{3,2,1,0:T(8,128)} %prev.1) | copy-start | bytes 786436
  1.7 0.9 %copy-start.1 = (f32[1,4,64,256]{3,2,1,0:T(8,128)S(1)}, f32[1,4,64,256]{3,2,1,0:T(8,128)}, u32[]{:S(2)}) copy-start(f32[1,4,64,256]{3,2,1,0:T(8,128)} %cur.1) | copy-start | bytes 786436
  2.6 0.9 %copy-start.2 = (f32[4,16,512]{2,1,0:T(8,128)S(1)}, f32[4,16,512]{2,1,0:T(8,128)}, u32[]{:S(2)}) copy-start(f32[4,16,512]{2,1,0:T(8,128)} %model.1) | copy-start | bytes 393220
  3.5 0.8 copy-start.3
  4.4 0.7 copy-start.4

commit v2 on v1

--- a/solution.py
+++ b/solution.py
@@ -2,6 +2,7 @@
 
 import jax
 import jax.numpy as jnp
+import numpy as np
 from jax import lax
 from jax.experimental import pallas as pl
 from jax.experimental.pallas import tpu as pltpu
@@ -26,8 +27,10 @@
 ROWS = 16
 HALO = 16
 OWN = 32
-CHUNK = 512
+CHUNK = 256
 PAD = 8
+RING = 14
+FIRST = 3
 
 
 def iota(shape, dim):
@@ -44,30 +47,44 @@
     def pick(tiles, k):
         return tiles[k] if 0 <= k < 2 else zero
 
-    half = lane - at if at <= 64 else lane - at + LANES
     if at <= 64:
         low = pick(first, tile)
         in_low = (lane >= at) & (lane < at + 64)
-        own = (lane + 64) % LANES
-        high = jnp.where(own >= at, pick(second, tile), pick(second, tile + 1))
-        if at == 0:
-            high = pick(second, tile)
+        high = pick(second, tile)
     else:
         low = jnp.where(lane >= at, pick(first, tile), pick(first, tile + 1))
         in_low = (lane >= at) | (lane < at - 64)
         own = (lane + 64) % LANES
         high = jnp.where(own >= at, pick(second, tile), pick(second, tile + 1))
-    del half
     both = jnp.where(in_low, low, high)
     return pltpu.roll(both, (LANES - at) % LANES, 1) if at else both
 
 
+def make_bands(bands):
+    r, c = iota((LANES, LANES), 0), iota((LANES, LANES), 1)
+    distance = jnp.where((r < 64) == (c < 64), jnp.abs(r - c), LANES)
+    main = jnp.zeros((LANES, LANES), F32)
+    rest = main
+    for k, weight in enumerate(stencil_weights):
+        rounded = float(np.float32(weight).astype(BF16))
+        main = jnp.where(distance == k, rounded, main)
+        rest = jnp.where(distance == k, float(np.float32(weight)) - rounded, rest)
+    swap = (jnp.abs(r - c) == 64).astype(F32).astype(BF16)
+    for half in range(2):
+        bands[pl.ds(LANES * half, LANES), pl.ds(0, LANES)] = main.astype(BF16)
+        bands[pl.ds(LANES * half, LANES), pl.ds(LANES, LANES)] = swap
+    bands[pl.ds(2 * LANES, LANES), pl.ds(0, LANES)] = rest.astype(BF16)
+    bands[pl.ds(2 * LANES, LANES), pl.ds(LANES, LANES)] = jnp.zeros((LANES, LANES), BF16)
+
+
 def kernel(
     near,
-    offx, offy, pulse, place, model, prev, cur, listing, record,
+    offx, offy, pulse, place, model_in, prev_in, cur_in, listing_in, record_in,
     out,
-    gathered, stage, fields, lams, shifted, onto, summed_r, windows, arrived, speeds, c2v, first_lap, accels, partial,
-    packed, outgoing, landed, placed, totals, ring_p, ring_m,
+    model, prev, cur, listing, record,
+    gathered, stage, fields, lams, bands, along_y, halves, onto, summed_r, windows, arrived, speeds, c2v, first_lap,
+    accels, partial, packed, outgoing, landed, placed, totals, ring_p, ring_m,
+    in_sems,
     gp_send, gp_recv, gm_send, gm_recv, ck_send, ck_recv, w_send, w_recv, o_send, o_recv,
     rp_send, rp_recv, rm_send, rm_recv,
 ):
@@ -85,6 +102,16 @@
     def device(k):
         return (LOCAL * level + lax.div(k, PARTS), lax.rem(k, PARTS))
 
+    inputs = [
+        pltpu.make_async_copy(model_in, model, in_sems.at[0]),
+        pltpu.make_async_copy(cur_in, cur, in_sems.at[1]),
+        pltpu.make_async_copy(prev_in, prev, in_sems.at[2]),
+        pltpu.make_async_copy(listing_in, listing, in_sems.at[3]),
+        pltpu.make_async_copy(record_in, record, in_sems.at[4]),
+    ]
+    for copy in inputs:
+        copy.start()
+
     barrier = pltpu.get_barrier_semaphore()
 
     def greet(k, carry):
@@ -95,9 +122,12 @@
         pl.semaphore_signal(barrier, inc=1, device_id=(LOCAL * other + group, part), device_id_type=MESH)
     lax.fori_loop(1, peers, greet, 0)
 
+    make_bands(bands)
+    inputs[0].wait()
     for tile in range(4):
         gathered[level, :, tile] = model[:, :, pl.ds(LANES * tile, LANES)]
     for which, source in ((0, cur), (1, prev)):
+        inputs[1 + which].wait()
         for i in range(2):
             low = [source[0, i, :, pl.ds(LANES * k, LANES)] for k in range(2)]
             high = [pltpu.roll(source[0, 2 + i, :, pl.ds(LANES * k, LANES)], 64, 1) for k in range(2)]
@@ -107,9 +137,9 @@
     pl.semaphore_wait(barrier, peers + 1)
 
     def ring_copy(m, sign, send, recv):
-        origin = lax.rem(level + near - sign * lax.div(m, 2) + near, near)
-        chunk = lax.rem(m, 2) if sign > 0 else 1 - lax.rem(m, 2)
-        where = gathered.at[origin, pl.ds(2 * chunk, 2)]
+        origin = lax.rem(level + near - sign * lax.div(m, 4) + near, near)
+        chunk = lax.rem(m + (0 if sign > 0 else 2), 4)
+        where = gathered.at[origin, chunk]
         to = up if sign > 0 else down
         return pltpu.make_async_remote_copy(
             src_ref=where, dst_ref=where, send_sem=send.at[m], recv_sem=recv.at[m],
@@ -117,9 +147,9 @@
         )
 
     def ring_wait(m, sign, send, recv):
-        origin = lax.rem(level + near - sign * (lax.div(m, 2) + 1) + near, near)
-        chunk = lax.rem(m, 2) if sign > 0 else 1 - lax.rem(m, 2)
-        where = gathered.at[origin, pl.ds(2 * chunk, 2)]
+        origin = lax.rem(level + near - sign * (lax.div(m, 4) + 1) + near, near)
+        chunk = lax.rem(m + (0 if sign > 0 else 2), 4)
+        where = gathered.at[origin, chunk]
         to = up if sign > 0 else down
         pltpu.make_async_remote_copy(
             src_ref=where, dst_ref=where, send_sem=send.at[m], recv_sem=recv.at[m],
@@ -134,10 +164,9 @@
             device_id=(shot, to), device_id_type=MESH,
         )
 
-    ring_copy(0, 1, gp_send, gp_recv).start()
-    ring_copy(0, -1, gm_send, gm_recv).start()
-    ring_copy(1, 1, gp_send, gp_recv).start()
-    ring_copy(1, -1, gm_send, gm_recv).start()
+    for m in range(4):
+        ring_copy(m, 1, gp_send, gp_recv).start()
+        ring_copy(m, -1, gm_send, gm_recv).start()
 
     def ckpt_start(k, carry):
         to = lax.rem(part + k, PARTS)
@@ -147,6 +176,8 @@
 
     lax.fori_loop(1, PARTS, ckpt_start, 0)
 
+    for edge in (0, 1, PLANES + 2, PLANES + 3):
+        halves[edge] = jnp.zeros((SPAN, LANES), F32)
     for ref, slots in ((fields, 2), (lams, 3)):
         for slot in range(slots):
             for edge in (0, 1, PLANES + 2, PLANES + 3):
@@ -179,25 +210,38 @@
             onto[pl.ds(LANES * k, LANES), pl.ds(0, CHUNK)] = jnp.where(match, high, 0.0).astype(BF16)
             onto[pl.ds(LANES * k, LANES), pl.ds(CHUNK, CHUNK)] = jnp.where(match, rest, 0.0).astype(BF16)
         dims = (((1,), (1,)), ((), ()))
-        total = lax.dot_general(hot, onto[:, pl.ds(0, CHUNK)], dims, preferred_element_type=F32)
-        total = total + lax.dot_general(hot, onto[:, pl.ds(CHUNK, CHUNK)], dims, preferred_element_type=F32)
-        summed_r[...] += total
+        both = jnp.concatenate([hot, hot], axis=1)
+        summed_r[...] += lax.dot_general(both, onto[...], dims, preferred_element_type=F32)
 
     def ring_step(m, carry):
-        ring_wait(m - 2, 1, gp_send, gp_recv)
+        ring_wait(m - 4, 1, gp_send, gp_recv)
         ring_copy(m, 1, gp_send, gp_recv).start()
-        ring_wait(m - 2, -1, gm_send, gm_recv)
+        ring_wait(m - 4, -1, gm_send, gm_recv)
         ring_copy(m, -1, gm_send, gm_recv).start()
+        receivers(m - 4 + FIRST)
+        return carry
+
+    def no_ring(m, carry):
         receivers(m)
         return carry
 
-    def two_first(m, carry):
-        receivers(m)
-        return carry
-
-    lax.fori_loop(0, 2, two_first, 0)
-    lax.fori_loop(2, 7, ring_step, 0)
-    receivers(7)
+    inputs[3].wait()
+    inputs[4].wait()
+    lax.fori_loop(0, FIRST, no_ring, 0)
+    lax.fori_loop(4, RING, ring_step, 0)
+    lax.fori_loop(RING - 4 + FIRST, listing.shape[1] // CHUNK, no_ring, 0)
+
+    def prepare(field, slot):
+        value = field[slot, pl.ds(2, PLANES), pl.ds(PAD, SPAN)].reshape(PLANES * SPAN, LANES)
+        high = value.astype(BF16)
+        rest = (value - high.astype(F32)).astype(BF16)
+        dims = (((1,), (0,)), ((), ()))
+        main = lax.dot_general(
+            jnp.concatenate([high, rest], axis=1), bands[pl.ds(0, 2 * LANES)], dims, preferred_element_type=F32
+        )
+        minor = lax.dot_general(high, bands[pl.ds(2 * LANES, LANES), pl.ds(0, LANES)], dims, preferred_element_type=F32)
+        along_y[...] = (main[:, :LANES] + minor).reshape(PLANES, SPAN, LANES)
+        halves[pl.ds(2, PLANES)] = main[:, LANES:].reshape(PLANES, SPAN, LANES)
 
     def laplace(field, slot, e):
         result = []
@@ -206,33 +250,20 @@
         def own(k):
             return field[slot, at + k, pl.ds(PAD, SPAN)]
 
-        def other(k):
-            return shifted[at + k]
-
+        other = {k: jnp.where(lower, halves[at + k], halves[at + k + 2]) for k in (-2, -1, 0, 1)}
         along_z = (
-            ((own(1), other(-1)), (other(0), other(-2)), (other(1), own(-1)), (own(2), own(-2))),
-            ((other(0), own(0)), (other(1), other(-1)), (own(2), other(-2)), (own(3), own(-1))),
+            ((own(1), other[-1]), (other[0], other[-2]), (other[1], own(-1)), (own(2), own(-2))),
+            ((other[0], own(0)), (other[1], other[-1]), (own(2), other[-2]), (own(3), own(-1))),
         )
         for i in range(2):
-            middle = own(i)
-            total = 3.0 * stencil_weights[0] * middle
+            total = 2.0 * stencil_weights[0] * own(i) + along_y[at + i - 2]
             for k in range(1, 5):
                 some = along_z[i][k - 1][0] + along_z[i][k - 1][1]
                 some = some + field[slot, at + i, pl.ds(PAD + k, SPAN)]
                 some = some + field[slot, at + i, pl.ds(PAD - k, SPAN)]
-                some = some + pltpu.roll(middle, k, 1)
-                some = some + pltpu.roll(middle, LANES - k, 1)
                 total = total + stencil_weights[k] * some
             result.append(total)
         return result
-
-    def shift(field, slot):
-        def one(p, carry):
-            both = jnp.where(lower, field[slot, p + 2, pl.ds(PAD, SPAN)], field[slot, p, pl.ds(PAD, SPAN)])
-            shifted[p] = pltpu.roll(both, 64, 1)
-            return carry
-
-        lax.fori_loop(0, PLANES + 2, one, 0)
 
     def residual(k, p):
         return summed_r[pl.ds(pl.multiple_of(p * SPAN, SPAN), SPAN), pl.ds(LANES * k, LANES)]
@@ -252,7 +283,7 @@
     lax.fori_loop(1, PARTS, ckpt_wait, 0)
 
     def keep_lap(field, slot, which):
-        shift(field, slot)
+        prepare(field, slot)
 
         def one(e, carry):
             for i, value in enumerate(laplace(field, slot, e)):
@@ -264,7 +295,7 @@
     keep_lap(fields, 0, 0)
     keep_lap(lams, 0, 1)
 
-    for m in (5, 6):
+    for m in range(RING - 4, RING):
         ring_wait(m, 1, gp_send, gp_recv)
         ring_wait(m, -1, gm_send, gm_recv)
 
@@ -347,7 +378,7 @@
     for n in range(STEPS):
         now, old = n % 2, 1 - n % 2
         if n:
-            shift(fields, now)
+            prepare(fields, now)
 
         def forward(e, carry, n=n, now=now, old=old):
             laps = laplace(fields, now, e) if n else [first_lap[0, 2 * e + i] for i in range(2)]
@@ -374,7 +405,7 @@
     for k in range(1, STEPS):
         now, old, new = (k - 1) % 3, (k - 2) % 3, k % 3
         if k > 1:
-            shift(lams, now)
+            prepare(lams, now)
 
         def adjoint(e, carry, k=k, now=now, old=old, new=new):
             laps = laplace(lams, now, e) if k > 1 else [first_lap[1, 2 * e + i] for i in range(2)]
@@ -461,45 +492,43 @@
 
     half = near // 2
 
-    def sum_chunk(m, sign):
-        odd = m % 2
-        return odd if sign > 0 else 1 - odd
+    def sum_place(m, sign):
+        pair = m // 2
+        plane = (pair % 2 * 2 + m % 2 + (0 if sign > 0 else 2)) % 4
+        return lax.rem(level + near + sign * (half - (pair + 1) // 2), near), plane
 
     def sum_copy(m, sign, ring, send, recv):
-        target = lax.rem(level + near + sign * (half - (m + 1) // 2), near)
         to = up if sign > 0 else down
         return pltpu.make_async_remote_copy(
-            src_ref=totals.at[target, pl.ds(2 * sum_chunk(m, sign), 2)], dst_ref=ring.at[m],
+            src_ref=totals.at[sum_place(m, sign)], dst_ref=ring.at[m],
             send_sem=send.at[m], recv_sem=recv.at[m],
             device_id=(LOCAL * to + group, part), device_id_type=MESH,
         )
 
     ways = ((1, ring_p, rp_send, rp_recv), (-1, ring_m, rm_send, rm_recv))
-    for m in range(near - 1):
+    for m in range(RING):
         for sign, ring, send, recv in ways:
-            if m >= 2:
-                sum_copy(m - 2, sign, ring, send, recv).wait_recv()
-                target = lax.rem(level + near + sign * (half - (m + 1) // 2), near)
-                where = pl.ds(2 * sum_chunk(m, sign), 2)
-                totals[target, where] = totals[target, where] + ring[m - 2]
+            if m >= 4:
+                sum_copy(m - 4, sign, ring, send, recv).wait_recv()
+                target, plane = sum_place(m, sign)
+                totals[target, plane] = totals[target, plane] + ring[m - 4]
             sum_copy(m, sign, ring, send, recv).start()
-    for m in (near - 3, near - 2):
+    for m in range(RING - 4, RING):
         for sign, ring, send, recv in ways:
             sum_copy(m, sign, ring, send, recv).wait_recv()
-    for c in range(2):
-        where = pl.ds(2 * c, 2)
-        total = totals[level, where]
+    for plane in range(4):
+        total = totals[level, plane]
         for sign, ring, send, recv in ways:
-            for m in (near - 3, near - 2):
-                if sum_chunk(m, sign) == c:
+            for m in range(RING - 4, RING):
+                if sum_place(m, sign)[1] == plane:
                     total = total + ring[m]
-        speed = model[where]
-        total = jnp.concatenate([total[:, tile] for tile in range(4)], axis=-1)
+        speed = model[plane]
+        total = jnp.concatenate([total[tile] for tile in range(4)], axis=-1)
         scaling = (speed - lower_bound) * (upper_bound - speed) / (upper_bound - lower_bound)
         limit = barrier_weight / (upper_bound - speed) - barrier_weight / (speed - lower_bound)
-        out[where] = scaling * (total + limit)
-
-    for m in range(near - 1):
+        out[plane] = scaling * (total + limit)
+
+    for m in range(RING):
         ring_copy(m, 1, gp_send, gp_recv).wait_send()
         ring_copy(m, -1, gm_send, gm_recv).wait_send()
         for sign, ring, send, recv in ways:
@@ -532,14 +561,17 @@
     return pl.pallas_call(
         functools.partial(kernel, near),
         out_shape=jax.ShapeDtypeStruct(model.shape, F32),
-        in_specs=[smem] * 4 + [vmem] * 5,
+        in_specs=[smem] * 4 + [pl.BlockSpec(memory_space=pltpu.HBM)] * 5,
         out_specs=vmem,
         scratch_shapes=[
+            *(pltpu.VMEM(a.shape, a.dtype) for a in (model, ckpt_prev, ckpt_cur, receivers, traces)),
             pltpu.VMEM((near, 4, 4, ROWS, LANES), F32),
             pltpu.VMEM((2, PARTS, 2, SPAN, LANES), F32),
             pltpu.VMEM((2,) + padded, F32),
             pltpu.VMEM((3,) + padded, F32),
-            pltpu.VMEM((PLANES + 2, SPAN, LANES), F32),
+            pltpu.VMEM((3 * LANES, 2 * LANES), BF16),
+            pltpu.VMEM(plain, F32),
+            pltpu.VMEM((PLANES + 4, SPAN, LANES), F32),
             pltpu.VMEM((STEPS * LANES, 2 * CHUNK), BF16),
             pltpu.VMEM((PLANES * SPAN, STEPS * LANES), F32),
             pltpu.VMEM((peers, 2, ROWS, LANES), F32),
@@ -554,12 +586,13 @@
             pltpu.VMEM((peers, ROWS, LANES), F32),
             pltpu.VMEM((LOCAL, 4, 6, ROWS, LANES), F32),
             pltpu.VMEM((near, 4, 4, ROWS, LANES), F32),
-            pltpu.VMEM((near - 1, 2, 4, ROWS, LANES), F32),
-            pltpu.VMEM((near - 1, 2, 4, ROWS, LANES), F32),
-            dma((near - 1,)), dma((near - 1,)), dma((near - 1,)), dma((near - 1,)),
+            pltpu.VMEM((RING, 4, ROWS, LANES), F32),
+            pltpu.VMEM((RING, 4, ROWS, LANES), F32),
+            dma((5,)),
+            dma((RING,)), dma((RING,)), dma((RING,)), dma((RING,)),
             dma((2, PARTS)), dma((2, PARTS)),
             dma((peers,)), dma((peers,)), dma((peers,)), dma((peers,)),
-            dma((near - 1,)), dma((near - 1,)), dma((near - 1,)), dma((near - 1,)),
+            dma((RING,)), dma((RING,)), dma((RING,)), dma((RING,)),
         ],
         compiler_params=pltpu.CompilerParams(
             collective_id=0, has_side_effects=True, vmem_limit_bytes=48 * 1024 * 1024

time: 88.8 us -> 74.6 us (0.84)
  Pallas kernels: 82.8 us -> 68.6 us
    pallas_call x1, Pallas kernels: 82.8 us -> 68.6 us  [on_device(): pl.pallas_call(functools.partial(kernel, near), out_shape=jax.ShapeDtypeS...]
where the time goes in v2:
time: 74.6 us; the launch traced here: 74.4 us
  Pallas kernels  68.6 us (92%)
  local copies, waits for them, and re-layouts  5.02 us (7%)
    pallas_call x1, Pallas kernels, on_device(): pl.pallas_call(functools.partial(kernel, near), out_shape=jax.ShapeDtypeS...  68.6 us
    unnamed x17, local copies, waits for them, and re-layouts  5.02 us

profile of v2, /device:TPU:4, one launch (start us, length us, event | category | flops | bytes accessed | tf_op | source)
XLA Modules:
  0.0 74.4 jit_solution(8038576733183593921)
XLA Ops:
  0.0 0.0 copy-start.7
  0.0 0.0 copy-start.6
  0.0 0.0 copy-start.5
  0.7 0.0 copy-done.7
  0.7 0.0 copy-done.6
  0.7 0.0 copy-done.5
  0.7 0.0 copy-start
  0.7 0.9 %copy-done = f32[1,4,64,256]{3,2,1,0:T(8,128)S(1)} copy-done((f32[1,4,64,256]{3,2,1,0:T(8,128)S(1)}, f32[1,4,64,256]{3,2,1,0:T(8,128)}, u32[]{:S(2)}) %copy-start) | copy-done | bytes 262168
  1.7 0.0 copy-start.1
  1.7 0.9 %copy-done.1 = f32[1,4,64,256]{3,2,1,0:T(8,128)S(1)} copy-done((f32[1,4,64,256]{3,2,1,0:T(8,128)S(1)}, f32[1,4,64,256]{3,2,1,0:T(8,128)}, u32[]{:S(2)}) %copy-start.1) | copy-done | bytes 262168
  2.6 0.0 copy-start.2
  2.6 0.9 %copy-done.2 = f32[4,16,512]{2,1,0:T(8,128)S(1)} copy-done((f32[4,16,512]{2,1,0:T(8,128)S(1)}, f32[4,16,512]{2,1,0:T(8,128)}, u32[]{:S(2)}) %copy-start.2) | copy-done | bytes 131096
  3.5 0.0 copy-start.3
  3.5 0.8 %copy-done.3 = f32[1,4,4096]{2,1,0:T(4,128)S(1)} copy-done((f32[1,4,4096]{2,1,0:T(4,128)S(1)}, f32[1,4,4096]{2,1,0:T(4,128)}, u32[]{:S(2)}) %copy-start.3) | copy-done | bytes 65560
  4.4 0.0 copy-start.4
  4.4 0.7 copy-done.4
  5.1 68.6 %shard_map.91 = f32[4,16,512]{2,1,0:T(8,128)S(1)} custom-call(s32[32]{0:T(128)S(1)} %copy-done.5, s32[32]{0:T(128)S(1)} %copy-done.6, f32[1,4]{1,0:T(1,128)S(1)} %copy-done.7, s32[1]{0:T(128)S(6)} %copy.11.place, f32[4,16,512]{2,1,0:T(8,128)S(1)} %copy-done.2, f32[1,4,64,256]{3,2,1,0:T(8,128)S(1)} %copy-done, f32[1,4,64,256]{3,2,1,0:T(8,128)S(1)} %copy-done.1, ...), custom_call_target="tpu_custom_call" | custom-call | tf_op jit(solution)/shard_map/pallas_call | solution.py:561
  73.7 0.7 copy.12
Async XLA Ops:
  0.0 0.7 copy-start.7
  0.0 0.7 copy-start.6
  0.0 0.7 copy-start.5
  0.7 1.0 %copy-start = (f32[1,4,64,256]{3,2,1,0:T(8,128)S(1)}, f32[1,4,64,256]{3,2,1,0:T(8,128)}, u32[]{:S(2)}) copy-start(f32[1,4,64,256]{3,2,1,0:T(8,128)} %prev_in.1) | copy-start | bytes 786436
  1.7 0.9 %copy-start.1 = (f32[1,4,64,256]{3,2,1,0:T(8,128)S(1)}, f32[1,4,64,256]{3,2,1,0:T(8,128)}, u32[]{:S(2)}) copy-start(f32[1,4,64,256]{3,2,1,0:T(8,128)} %cur_in.1) | copy-start | bytes 786436
  2.6 0.9 %copy-start.2 = (f32[4,16,512]{2,1,0:T(8,128)S(1)}, f32[4,16,512]{2,1,0:T(8,128)}, u32[]{:S(2)}) copy-start(f32[4,16,512]{2,1,0:T(8,128)} %model_in.1) | copy-start | bytes 393220
  3.5 0.8 %copy-start.3 = (f32[1,4,4096]{2,1,0:T(4,128)S(1)}, f32[1,4,4096]{2,1,0:T(4,128)}, u32[]{:S(2)}) copy-start(f32[1,4,4096]{2,1,0:T(4,128)} %record_in.1) | copy-start | bytes 196612
  4.4 0.7 copy-start.4

commit v3 on v2

v3 whole, which is shorter than its diff:
```python
import functools

import jax
import jax.numpy as jnp
import numpy as np
from jax import lax
from jax.experimental import pallas as pl
from jax.experimental.pallas import tpu as pltpu
from jax.sharding import PartitionSpec as P

MESH = pl.DeviceIdType.MESH
F32 = jnp.float32
BF16 = jnp.bfloat16
STEPS = 4

stencil_weights = (-205.0 / 72.0, 8.0 / 5.0, -1.0 / 5.0, 8.0 / 315.0, -1.0 / 560.0)
courant = 0.095
lower_bound = 1.0
upper_bound = 5.0
barrier_weight = 0.5

PARTS = 8
LOCAL = 4
PLANES = 16
SPAN = 64
LANES = 128
ROWS = 16
HALO = 16
OWN = 32
CHUNK = 256
PAD = 8
FAR_FIRST = (4, 3, 5, 2, 6, 1, 7)
FIRST = 7


def iota(shape, dim):
    return lax.broadcasted_iota(jnp.int32, shape, dim)


def window(first, second, part):
    rows = first[0].shape[0]
    lane = iota((rows, LANES), 1)
    zero = jnp.zeros((rows, LANES), F32)
    start = OWN * part - HALO
    tile, at = start // LANES, start % LANES

    def pick(tiles, k):
        return tiles[k] if 0 <= k < 2 else zero

    if at <= 64:
        low = pick(first, tile)
        in_low = (lane >= at) & (lane < at + 64)
        high = pick(second, tile)
    else:
        low = jnp.where(lane >= at, pick(first, tile), pick(first, tile + 1))
        in_low = (lane >= at) | (lane < at - 64)
        own = (lane + 64) % LANES
        high = jnp.where(own >= at, pick(second, tile), pick(second, tile + 1))
    both = jnp.where(in_low, low, high)
    return pltpu.roll(both, (LANES - at) % LANES, 1) if at else both


def make_bands(bands):
    r, c = iota((LANES, LANES), 0), iota((LANES, LANES), 1)
    distance = jnp.where((r < 64) == (c < 64), jnp.abs(r - c), LANES)
    main = jnp.zeros((LANES, LANES), F32)
    rest = main
    for k, weight in enumerate(stencil_weights):
        rounded = float(np.float32(weight).astype(BF16))
        main = jnp.where(distance == k, rounded, main)
        rest = jnp.where(distance == k, float(np.float32(weight)) - rounded, rest)
    swap = (jnp.abs(r - c) == 64).astype(F32).astype(BF16)
    for half in range(2):
        bands[pl.ds(LANES * half, LANES), pl.ds(0, LANES)] = main.astype(BF16)
        bands[pl.ds(LANES * half, LANES), pl.ds(LANES, LANES)] = swap
    bands[pl.ds(2 * LANES, LANES), pl.ds(0, LANES)] = rest.astype(BF16)
    bands[pl.ds(2 * LANES, LANES), pl.ds(LANES, LANES)] = jnp.zeros((LANES, LANES), BF16)


def kernel(
    near,
    offx, offy, pulse, place, model_in, prev_in, cur_in, listing_in, record_in,
    out,
    model, prev, cur, listing, record,
    m_out, cyclic, rows_out, rows_in, rows_16, stage, fields, lams, bands, along_y, halves, onto, summed_r, windows, arrived, speeds, c2v, first_lap,
    accels, partial, packed, outgoing, z_out, z_in, outgoing_2, landed, by_shot, placed, totals, sums, final,
    in_sems,
    m_send, m_recv, r_send, r_recv, ck_send, ck_recv, w_send, w_recv, o_send, o_recv,
    z_send, z_recv, s_send, s_recv,
):
    shot = lax.axis_index("shots")
    part = lax.axis_index("depth")
    level = lax.div(shot, LOCAL)
    group = lax.rem(shot, LOCAL)
    me = group * PARTS + part
    peers = LOCAL * PARTS
    lane = iota((SPAN, LANES), 1)
    lower = lane < 64

    def along(step):
        return lax.rem(level + step, near)

    def device(k):
        return (LOCAL * level + lax.div(k, PARTS), lax.rem(k, PARTS))

    inputs = [
        pltpu.make_async_copy(model_in, model, in_sems.at[0]),
        pltpu.make_async_copy(cur_in, cur, in_sems.at[1]),
        pltpu.make_async_copy(prev_in, prev, in_sems.at[2]),
        pltpu.make_async_copy(listing_in, listing, in_sems.at[3]),
        pltpu.make_async_copy(record_in, record, in_sems.at[4]),
    ]
    for copy in inputs:
        copy.start()

    barrier = pltpu.get_barrier_semaphore()

    def greet(k, carry):
        pl.semaphore_signal(barrier, inc=1, device_id=device(lax.rem(me + k, peers)), device_id_type=MESH)
        return carry

    for step in FAR_FIRST:
        pl.semaphore_signal(barrier, inc=1, device_id=(LOCAL * along(step) + group, part), device_id_type=MESH)
    lax.fori_loop(1, peers, greet, 0)

    make_bands(bands)
    inputs[0].wait()
    for to in range(near):
        for tile in range(4):
            for plane in range(4):
                m_out[to, tile, pl.ds(2 * plane, 2)] = model[plane, pl.ds(2 * to, 2), pl.ds(LANES * tile, LANES)]
    for which, source in ((0, cur), (1, prev)):
        inputs[1 + which].wait()
        for i in range(2):
            low = [source[0, i, :, pl.ds(LANES * k, LANES)] for k in range(2)]
            high = [pltpu.roll(source[0, 2 + i, :, pl.ds(LANES * k, LANES)], 64, 1) for k in range(2)]
            for to in range(PARTS):
                stage[which, to, i] = window(low, high, to)

    pl.semaphore_wait(barrier, peers - 1 + len(FAR_FIRST))

    def model_copy(to, origin):
        return pltpu.make_async_remote_copy(
            src_ref=m_out.at[to], dst_ref=cyclic.at[origin],
            send_sem=m_send.at[to], recv_sem=m_recv.at[origin],
            device_id=(LOCAL * to + group, part), device_id_type=MESH,
        )

    def rows_copy(to, origin):
        return pltpu.make_async_remote_copy(
            src_ref=rows_out.at[to], dst_ref=rows_in.at[pl.ds(SPAN * origin, SPAN)],
            send_sem=r_send.at[to], recv_sem=r_recv.at[origin],
            device_id=(LOCAL * to + group, part), device_id_type=MESH,
        )

    def ckpt_copy(which, to, origin):
        return pltpu.make_async_remote_copy(
            src_ref=stage.at[which, to],
            dst_ref=fields.at[which, pl.ds(2 + 2 * origin, 2), pl.ds(PAD, SPAN)],
            send_sem=ck_send.at[which, to], recv_sem=ck_recv.at[which, origin],
            device_id=(shot, to), device_id_type=MESH,
        )

    for step in FAR_FIRST:
        model_copy(along(step), level).start()
    cyclic[level] = m_out[level]

    def ckpt_start(k, carry):
        to = lax.rem(part + k, PARTS)
        ckpt_copy(0, to, part).start()
        ckpt_copy(1, to, part).start()
        return carry

    lax.fori_loop(1, PARTS, ckpt_start, 0)

    for edge in (0, 1, PLANES + 2, PLANES + 3):
        for which in range(2):
            halves[which, edge] = jnp.zeros((SPAN, LANES), F32)
    for ref, slots in ((fields, 2), (lams, 3)):
        for slot in range(slots):
            for edge in (0, 1, PLANES + 2, PLANES + 3):
                ref[slot, edge] = jnp.zeros((SPAN + 2 * PAD, LANES), F32)
            for edge in range(2, PLANES + 2):
                ref[slot, edge, pl.ds(0, PAD)] = jnp.zeros((PAD, LANES), F32)
                ref[slot, edge, pl.ds(PAD + SPAN, PAD)] = jnp.zeros((PAD, LANES), F32)
    for which in range(2):
        fields[which, pl.ds(2 + 2 * part, 2), pl.ds(PAD, SPAN)] = stage[which, part]
    for tile in (0, 1, 5):
        placed[:, tile] = jnp.zeros((LOCAL * near, 8, LANES), F32)

    summed_r[...] = jnp.zeros(summed_r.shape, F32)

    def receivers(step):
        at = pl.ds(pl.multiple_of(step * CHUNK, CHUNK), CHUNK)
        flat = listing[:, at]
        zc = lax.shift_right_logical(flat, 14)
        x = lax.shift_right_logical(flat, 8) & 63
        y = (flat & 255) - (OWN * part - HALO)
        row = (lax.shift_right_logical(zc, 2) * 2 + (zc & 1)) * SPAN + x
        column = jnp.where((y >= 0) & (y < 64), (lax.shift_right_logical(zc, 1) & 1) * 64 + y, -1)
        hot = (iota((PLANES * SPAN, CHUNK), 0) == row).astype(F32).astype(BF16)
        match = iota((LANES, CHUNK), 0) == column
        for k in range(STEPS):
            value = record[0, pl.ds(k, 1), at]
            high = value.astype(BF16).astype(F32)
            rest = value - high
            onto[pl.ds(LANES * k, LANES), pl.ds(0, CHUNK)] = jnp.where(match, high, 0.0).astype(BF16)
            onto[pl.ds(LANES * k, LANES), pl.ds(CHUNK, CHUNK)] = jnp.where(match, rest, 0.0).astype(BF16)
        dims = (((1,), (1,)), ((), ()))
        both = jnp.concatenate([hot, hot], axis=1)
        summed_r[...] += lax.dot_general(both, onto[...], dims, preferred_element_type=F32)

    def more(step, carry):
        receivers(step)
        return carry

    inputs[3].wait()
    inputs[4].wait()
    lax.fori_loop(0, FIRST, more, 0)

    for step in FAR_FIRST:
        model_copy(level, along(step)).wait_recv()

    tile_lane = iota((8, LANES), 1)
    odd = iota((8, LANES), 0) & 1

    def spot(shot_k):
        t = offx[shot_k] - (ROWS * group + 2 * level) + SPAN
        oy = offy[shot_k]
        return lax.shift_right_logical(t, 6) - 1, t & 63, lax.shift_right_logical(oy, 7), oy & 127

    def cut(step, carry):
        to = lax.rem(level + near + lax.div(near - step, 2) * (1 - 2 * lax.rem(step, 2)), near)
        for b in range(LOCAL):
            block, rest, tile, at = spot(LOCAL * to + b)
            upper_rows = odd >= rest
            q0, q1 = jnp.maximum(block, 0), jnp.minimum(block + 1, near - 1)
            back = lax.rem(LANES - at, LANES)
            keep = tile_lane < LANES - at
            turned = []
            for k in range(3):
                t = jnp.minimum(tile + k, 3)
                turned.append(pltpu.roll(jnp.where(upper_rows, cyclic[q0, t], cyclic[q1, t]), back, 1))
            for k in range(2):
                rows_out[to, pl.ds(8 * (2 * b + k), 8)] = jnp.where(keep, turned[k], turned[k + 1])
        @pl.when(to != level)
        def _():
            rows_copy(to, level).start()
        return carry

    lax.fori_loop(0, near, cut, 0)
    rows_in[pl.ds(pl.multiple_of(SPAN * level, SPAN), SPAN)] = rows_out[level]
    lax.fori_loop(FIRST, listing.shape[1] // CHUNK, more, 0)
    for step in FAR_FIRST:
        rows_copy(level, along(step)).wait_recv()

    def window_copy(to, origin):
        return pltpu.make_async_remote_copy(
            src_ref=windows.at[to],
            dst_ref=arrived.at[pl.ds(2 * lax.rem(origin, PARTS), 2), pl.ds(ROWS * lax.div(origin, PARTS), ROWS)],
            send_sem=w_send.at[to], recv_sem=w_recv.at[origin],
            device_id=device(to), device_id_type=MESH,
        )

    def share(b, carry):
        for plane in range(4):
            for k in range(2):
                for j in range(2):
                    rows_16[plane, k, pl.ds(j, 8, stride=2)] = (
                        rows_in[pl.ds(8 * (2 * b + k) + 2 * plane + j, 8, stride=SPAN)]
                    )
        for i in range(2):
            low = [rows_16[i, k] for k in range(2)]
            high = [pltpu.roll(rows_16[2 + i, k], 64, 1) for k in range(2)]
            for to in range(PARTS):
                windows[b * PARTS + to, i] = window(low, high, to)
        for to in range(PARTS):
            @pl.when(b * PARTS + to != me)
            def _():
                window_copy(b * PARTS + to, me).start()
        return carry

    lax.fori_loop(0, LOCAL, share, 0)
    arrived[pl.ds(2 * part, 2), pl.ds(ROWS * group, ROWS)] = windows[me]

    def prepare(field, slot, which):
        value = field[slot, pl.ds(2, PLANES), pl.ds(PAD, SPAN)].reshape(PLANES * SPAN, LANES)
        high = value.astype(BF16)
        rest = (value - high.astype(F32)).astype(BF16)
        dims = (((1,), (0,)), ((), ()))
        main = lax.dot_general(
            jnp.concatenate([high, rest], axis=1), bands[pl.ds(0, 2 * LANES)], dims, preferred_element_type=F32
        )
        minor = lax.dot_general(high, bands[pl.ds(2 * LANES, LANES), pl.ds(0, LANES)], dims, preferred_element_type=F32)
        along_y[which] = (main[:, :LANES] + minor).reshape(PLANES, SPAN, LANES)
        halves[which, pl.ds(2, PLANES)] = main[:, LANES:].reshape(PLANES, SPAN, LANES)

    def laplace(field, slot, which, e):
        result = []
        at = 2 + 2 * e

        def own(k):
            return field[slot, at + k, pl.ds(PAD, SPAN)]

        other = {k: jnp.where(lower, halves[which, at + k], halves[which, at + k + 2]) for k in (-2, -1, 0, 1)}
        along_z = (
            ((own(1), other[-1]), (other[0], other[-2]), (other[1], own(-1)), (own(2), own(-2))),
            ((other[0], own(0)), (other[1], other[-1]), (own(2), other[-2]), (own(3), own(-1))),
        )
        for i in range(2):
            total = 2.0 * stencil_weights[0] * own(i) + along_y[which, at + i - 2]
            for k in range(1, 5):
                some = along_z[i][k - 1][0] + along_z[i][k - 1][1]
                some = some + field[slot, at + i, pl.ds(PAD + k, SPAN)]
                some = some + field[slot, at + i, pl.ds(PAD - k, SPAN)]
                total = total + stencil_weights[k] * some
            result.append(total)
        return result

    def residual(k, p):
        return summed_r[pl.ds(pl.multiple_of(p * SPAN, SPAN), SPAN), pl.ds(LANES * k, LANES)]

    def to_lam(p, carry):
        lams[0, p + 2, pl.ds(PAD, SPAN)] = residual(0, p)
        return carry

    lax.fori_loop(0, PLANES, to_lam, 0)

    def ckpt_wait(k, carry):
        origin = lax.rem(part + k, PARTS)
        ckpt_copy(0, part, origin).wait_recv()
        ckpt_copy(1, part, origin).wait_recv()
        return carry

    lax.fori_loop(1, PARTS, ckpt_wait, 0)

    prepare(fields, 0, 0)
    prepare(lams, 0, 1)

    def first(e, carry):
        for which, field in ((0, fields), (1, lams)):
            for i, value in enumerate(laplace(field, 0, which, e)):
                first_lap[which, 2 * e + i] = value
        return carry

    lax.fori_loop(0, PARTS, first, 0)

    def window_wait(k, carry):
        window_copy(me, lax.rem(me + k, peers)).wait_recv()
        return carry

    lax.fori_loop(1, peers, window_wait, 0)

    turn = offx[shot] & 63

    def make_c2v(p, carry):
        arrived[p, pl.ds(SPAN, SPAN)] = arrived[p, pl.ds(0, SPAN)]
        speed = arrived[p, pl.ds(turn, SPAN)]
        speeds[p] = speed
        scaled = courant * speed
        c2v[p] = scaled * scaled
        return carry

    lax.fori_loop(0, PLANES, make_c2v, 0)

    flat = place[0]
    zc = lax.shift_right_logical(flat, 14)
    sy = (flat & 255) - (OWN * part - HALO)
    s_plane = lax.shift_right_logical(zc, 2) * 2 + (zc & 1)
    s_lane = jnp.where((sy >= 0) & (sy < 64), (lax.shift_right_logical(zc, 1) & 1) * 64 + sy, -1)
    at_source = (lane == s_lane) & (iota((SPAN, LANES), 0) == (lax.shift_right_logical(flat, 8) & 63))

    def accel_of(value, p, n):
        strength = jnp.where(p == s_plane, pulse[0, n], 0.0)
        return c2v[p] * value + jnp.where(at_source, strength, 0.0)

    inner = pl.ds(PAD, SPAN)

    def step_loop(n):
        now, old = n % 2, 1 - n % 2
        if n:
            prepare(fields, now, 0)
            if n < STEPS - 1:
                prepare(lams, n, 1)

        def step(e, carry):
            laps = laplace(fields, now, 0, e) if n else [first_lap[0, 2 * e + i] for i in range(2)]
            accel = [accel_of(laps[i], 2 * e + i, n) for i in range(2)]
            if n < STEPS - 1:
                laps = laplace(lams, n, 1, e) if n else [first_lap[1, 2 * e + i] for i in range(2)]
            for i in range(2):
                p = 2 * e + i
                if n < STEPS - 1:
                    fields[old, p + 2, inner] = (
                        2.0 * fields[now, p + 2, inner] - fields[old, p + 2, inner] + accel[i]
                    )
                    lam = lams[n, p + 2, inner]
                    newer = 2.0 * lam + c2v[p] * laps[i] + residual(n + 1, p)
                    if n:
                        newer = newer - lams[n - 1, p + 2, inner]
                if n < STEPS - 2:
                    accels[n, p] = accel[i]
                    lams[n + 1, p + 2, inner] = newer
                elif n == STEPS - 2:
                    partial[p] = newer * accels[0, p] + lam * accels[1, p] + lams[1, p + 2, inner] * accel[i]
            if n == STEPS - 1:
                send_parts(e, [
                    (partial[2 * e + i] + lams[0, 2 * e + i + 2, inner] * accel[i]) * 2.0 / speeds[2 * e + i]
                    for i in range(2)
                ])
            return carry

        lax.fori_loop(0, PARTS, step, 0)

    def send_parts(e, parts):
        both = jnp.where((lane & 63) < OWN, pltpu.roll(parts[0], LANES - HALO, 1), pltpu.roll(parts[1], OWN - HALO, 1))
        packed[e, pl.ds(0, SPAN)] = both
        packed[e, pl.ds(SPAN, SPAN)] = both
        outgoing[e] = packed[e, pl.ds((SPAN - turn) & 63, SPAN)]
        for to in range(near):
            for j in range(2):
                z_out[to, pl.ds(8 * e + 4 * j, 4)] = outgoing[e, pl.ds(2 * to + j, 4, stride=ROWS)]

    for n in range(STEPS):
        step_loop(n)

    def z_copy(to, origin):
        return pltpu.make_async_remote_copy(
            src_ref=z_out.at[to], dst_ref=z_in.at[pl.ds(SPAN * origin, SPAN)],
            send_sem=z_send.at[to], recv_sem=z_recv.at[origin],
            device_id=(LOCAL * to + group, part), device_id_type=MESH,
        )

    for step in FAR_FIRST:
        z_copy(along(step), level).start()
    z_in[pl.ds(pl.multiple_of(SPAN * level, SPAN), SPAN)] = z_out[level]
    for step in FAR_FIRST:
        z_copy(level, along(step)).wait_recv()

    def out_copy(to, origin):
        return pltpu.make_async_remote_copy(
            src_ref=outgoing_2.at[to], dst_ref=landed.at[origin],
            send_sem=o_send.at[to], recv_sem=o_recv.at[origin],
            device_id=device(to), device_id_type=MESH,
        )

    def out_start(e, carry):
        for b in range(LOCAL):
            for j in range(2):
                outgoing_2[b * PARTS + e, pl.ds(8 * j, 8)] = z_in[pl.ds(8 * e + 4 * j + b, 8, stride=SPAN)]
            @pl.when(b * PARTS + e != me)
            def _():
                out_copy(b * PARTS + e, me).start()
        return carry

    lax.fori_loop(0, PARTS, out_start, 0)
    landed[me] = outgoing_2[me]

    def out_wait(k, carry):
        out_copy(me, lax.rem(me + k, peers)).wait_recv()
        return carry

    lax.fori_loop(1, peers, out_wait, 0)

    group_of = lax.shift_right_logical(tile_lane, 5)

    def put(b, carry):
        for j in range(2):
            for k in range(2):
                pieces = [landed[b * PARTS + 4 * k + c, pl.ds(8 * j, 8)] for c in range(4)]
                for plane in range(4):
                    total = None
                    for c in range(4):
                        by = (OWN * (c - plane)) % LANES
                        piece = pltpu.roll(pieces[c], by, 1) if by else pieces[c]
                        total = piece if total is None else jnp.where(group_of == c, piece, total)
                    by_shot[k, pl.ds(8 * (2 * plane + j), 8)] = total
        for z in range(near):
            at = offy[LOCAL * z + b] & 127
            keep = tile_lane >= at
            first, second = (pltpu.roll(by_shot[k, pl.ds(z, 8, stride=8)], at, 1) for k in range(2))
            placed[b * near + z, 2] = jnp.where(keep, first, 0.0)
            placed[b * near + z, 3] = jnp.where(keep, second, first)
            placed[b * near + z, 4] = jnp.where(keep, 0.0, second)
        return carry

    lax.fori_loop(0, LOCAL, put, 0)

    def add_up(k, sums):
        block, rest, tile, _ = spot(LOCAL * lax.rem(k, near) + lax.div(k, near))
        block = jnp.where(odd >= rest, block, block + 1)
        cells = placed[k, pl.ds(2 - tile, 4)]
        return tuple(total + jnp.where(block == q, cells, 0.0) for q, total in enumerate(sums))

    zero = jnp.zeros((4, 8, LANES), F32)
    for q, total in enumerate(lax.fori_loop(0, LOCAL * near, add_up, (zero,) * near)):
        totals[q] = total

    def sum_copy(to, origin):
        return pltpu.make_async_remote_copy(
            src_ref=totals.at[to], dst_ref=sums.at[origin],
            send_sem=s_send.at[to], recv_sem=s_recv.at[origin],
            device_id=(LOCAL * to + group, part), device_id_type=MESH,
        )

    for step in FAR_FIRST:
        sum_copy(along(step), level).start()
    sums[level] = totals[level]
    for step in FAR_FIRST:
        sum_copy(level, along(step)).wait_recv()
    for plane in range(4):
        for tile in range(4):
            for j in range(2):
                for z in range(near):
                    final[plane, tile, pl.ds(2 * z + j, 1)] = sums[z, tile, pl.ds(2 * plane + j, 1)]
        speed = model[plane]
        total = jnp.concatenate([final[plane, tile] for tile in range(4)], axis=-1)
        scaling = (speed - lower_bound) * (upper_bound - speed) / (upper_bound - lower_bound)
        limit = barrier_weight / (upper_bound - speed) - barrier_weight / (speed - lower_bound)
        out[plane] = scaling * (total + limit)

    for step in FAR_FIRST:
        model_copy(along(step), level).wait_send()
        rows_copy(along(step), level).wait_send()
        z_copy(along(step), level).wait_send()
        sum_copy(along(step), level).wait_send()

    def ckpt_sent(k, carry):
        to = lax.rem(part + k, PARTS)
        ckpt_copy(0, to, part).wait_send()
        ckpt_copy(1, to, part).wait_send()
        return carry

    lax.fori_loop(1, PARTS, ckpt_sent, 0)

    def blocks_sent(k, carry):
        to = lax.rem(me + k, peers)
        window_copy(to, me).wait_send()
        out_copy(to, me).wait_send()
        return carry

    lax.fori_loop(1, peers, blocks_sent, 0)


def on_device(near, model, offsets_x, offsets_y, ckpt_prev, ckpt_cur, wavelet, source, receivers, traces):
    peers = LOCAL * PARTS
    vmem = pl.BlockSpec(memory_space=pltpu.VMEM)
    smem = pl.BlockSpec(memory_space=pltpu.SMEM)
    padded = (PLANES + 4, SPAN + 2 * PAD, LANES)
    plain = (PLANES, SPAN, LANES)
    dma = pltpu.SemaphoreType.DMA
    return pl.pallas_call(
        functools.partial(kernel, near),
        out_shape=jax.ShapeDtypeStruct(model.shape, F32),
        in_specs=[smem] * 4 + [pl.BlockSpec(memory_space=pltpu.HBM)] * 5,
        out_specs=vmem,
        scratch_shapes=[
            *(pltpu.VMEM(a.shape, a.dtype) for a in (model, ckpt_prev, ckpt_cur, receivers, traces)),
            pltpu.VMEM((near, 4, 8, LANES), F32),
            pltpu.VMEM((near, 4, 8, LANES), F32),
            pltpu.VMEM((near, SPAN, LANES), F32),
            pltpu.VMEM((near * SPAN, LANES), F32),
            pltpu.VMEM((4, 2, ROWS, LANES), F32),
            pltpu.VMEM((2, PARTS, 2, SPAN, LANES), F32),
            pltpu.VMEM((2,) + padded, F32),
            pltpu.VMEM((3,) + padded, F32),
            pltpu.VMEM((3 * LANES, 2 * LANES), BF16),
            pltpu.VMEM((2,) + plain, F32),
            pltpu.VMEM((2, PLANES + 4, SPAN, LANES), F32),
            pltpu.VMEM((STEPS * LANES, 2 * CHUNK), BF16),
            pltpu.VMEM((PLANES * SPAN, STEPS * LANES), F32),
            pltpu.VMEM((peers, 2, ROWS, LANES), F32),
            pltpu.VMEM((PLANES, 2 * SPAN, LANES), F32),
            pltpu.VMEM(plain, F32),
            pltpu.VMEM(plain, F32),
            pltpu.VMEM((2,) + plain, F32),
            pltpu.VMEM((2,) + plain, F32),
            pltpu.VMEM(plain, F32),
            pltpu.VMEM((PARTS, 2 * SPAN, LANES), F32),
            pltpu.VMEM((PARTS, SPAN, LANES), F32),
            pltpu.VMEM((near, SPAN, LANES), F32),
            pltpu.VMEM((near * SPAN, LANES), F32),
            pltpu.VMEM((peers, ROWS, LANES), F32),
            pltpu.VMEM((peers, ROWS, LANES), F32),
            pltpu.VMEM((2, SPAN, LANES), F32),
            pltpu.VMEM((LOCAL * near, 6, 8, LANES), F32),
            pltpu.VMEM((near, 4, 8, LANES), F32),
            pltpu.VMEM((near, 4, 8, LANES), F32),
            pltpu.VMEM((4, 4, ROWS, LANES), F32),
            dma((5,)),
            dma((near,)), dma((near,)), dma((near,)), dma((near,)),
            dma((2, PARTS)), dma((2, PARTS)),
            dma((peers,)), dma((peers,)), dma((peers,)), dma((peers,)),
            dma((near,)), dma((near,)), dma((near,)), dma((near,)),
        ],
        compiler_params=pltpu.CompilerParams(
            collective_id=0, has_side_effects=True, vmem_limit_bytes=62 * 1024 * 1024
        ),
    )(offsets_x, offsets_y, wavelet, source, model, ckpt_prev, ckpt_cur, receivers, traces)


def solution(mesh):
    placed = (
        P("depth", "shots", None),
        P(),
        P(),
        P("shots", "depth", None, None),
        P("shots", "depth", None, None),
        P("shots", None),
        P("shots"),
        P("shots", None),
        P("shots", None, None),
    )
    near = mesh.shape["shots"] // LOCAL
    return jax.shard_map(
        functools.partial(on_device, near),
        mesh=mesh, in_specs=placed, out_specs=P("depth", "shots", None), check_vma=False,
    )
```

time: 74.6 us -> 68.4 us (0.917)
  the two profiles are of different devices: /device:TPU:4 before, /device:TPU:1 now
where the time goes in v3:
time: 68.4 us; the launch traced here: 68.3 us
  Pallas kernels  66 us (96%)
  local copies, waits for them, and re-layouts  1.57 us (2%)
    pallas_call x1, Pallas kernels, on_device(): pl.pallas_call(functools.partial(kernel, near), out_shape=jax.ShapeDtypeS...  66 us
    unnamed x1, local copies, waits for them, and re-layouts  1.57 us

profile of v3, /device:TPU:1, one launch (start us, length us, event | category | flops | bytes accessed | tf_op | source)
XLA Modules:
  0.0 68.3 jit_solution(2698274811972222899)
XLA Ops:
  0.7 66.0 %shard_map.91 = f32[4,16,512]{2,1,0:T(8,128)} custom-call(s32[32]{0:T(128)} %offx.1, s32[32]{0:T(128)} %offy.1, f32[1,4]{1,0:T(1,128)} %pulse.1, s32[1]{0:T(128)S(6)} %copy.11.place, f32[4,16,512]{2,1,0:T(8,128)} %model_in.1, f32[1,4,64,256]{3,2,1,0:T(8,128)} %prev_in.1, f32[1,4,64,256]{3,2,1,0:T(8,128)} %cur_in.1, s32[1,4096]{1,0:T(1,128)} %listing_in.1, ...), custom_call_target="tpu_custom_call" | custom-call | tf_op jit(solution)/shard_map/pallas_call | solution.py:552
  66.7 1.6 %copy.12 = f32[4,16,512]{2,1,0:T(8,128)} copy(f32[4,16,512]{2,1,0:T(8,128)} %shard_map.91) | data formatting | bytes 262144

commit v4 on v3

--- a/solution.py
+++ b/solution.py
@@ -30,7 +30,8 @@
 CHUNK = 256
 PAD = 8
 FAR_FIRST = (4, 3, 5, 2, 6, 1, 7)
-FIRST = 7
+FIRST = 4
+SECOND = 8
 
 
 def iota(shape, dim):
@@ -250,7 +251,7 @@
 
     lax.fori_loop(0, near, cut, 0)
     rows_in[pl.ds(pl.multiple_of(SPAN * level, SPAN), SPAN)] = rows_out[level]
-    lax.fori_loop(FIRST, listing.shape[1] // CHUNK, more, 0)
+    lax.fori_loop(FIRST, SECOND, more, 0)
     for step in FAR_FIRST:
         rows_copy(level, along(step)).wait_recv()
 
@@ -282,6 +283,7 @@
 
     lax.fori_loop(0, LOCAL, share, 0)
     arrived[pl.ds(2 * part, 2), pl.ds(ROWS * group, ROWS)] = windows[me]
+    lax.fori_loop(SECOND, listing.shape[1] // CHUNK, more, 0)
 
     def prepare(field, slot, which):
         value = field[slot, pl.ds(2, PLANES), pl.ds(PAD, SPAN)].reshape(PLANES * SPAN, LANES)
@@ -333,6 +335,17 @@
         return carry
 
     lax.fori_loop(1, PARTS, ckpt_wait, 0)
+
+    def ckpt_sent(k, carry):
+        to = lax.rem(part + k, PARTS)
+        ckpt_copy(0, to, part).wait_send()
+        ckpt_copy(1, to, part).wait_send()
+        return carry
+
+    lax.fori_loop(1, PARTS, ckpt_sent, 0)
+    for far in FAR_FIRST:
+        model_copy(along(far), level).wait_send()
+        rows_copy(along(far), level).wait_send()
 
     prepare(fields, 0, 0)
     prepare(lams, 0, 1)
@@ -410,7 +423,13 @@
                 ])
             return carry
 
-        lax.fori_loop(0, PARTS, step, 0)
+        if n < STEPS - 1:
+            lax.fori_loop(0, PARTS, step, 0)
+            return
+        for half in range(2):
+            lax.fori_loop(half * PARTS // 2, (half + 1) * PARTS // 2, step, 0)
+            for far in FAR_FIRST:
+                z_copy(along(far), level, half).start()
 
     def send_parts(e, parts):
         both = jnp.where((lane & 63) < OWN, pltpu.roll(parts[0], LANES - HALO, 1), pltpu.roll(parts[1], OWN - HALO, 1))
@@ -421,21 +440,17 @@
             for j in range(2):
                 z_out[to, pl.ds(8 * e + 4 * j, 4)] = outgoing[e, pl.ds(2 * to + j, 4, stride=ROWS)]
 
+    def z_copy(to, origin, half):
+        return pltpu.make_async_remote_copy(
+            src_ref=z_out.at[to, pl.ds(OWN * half, OWN)],
+            dst_ref=z_in.at[pl.ds(SPAN * origin + OWN * half, OWN)],
+            send_sem=z_send.at[half, to], recv_sem=z_recv.at[half, origin],
+            device_id=(LOCAL * to + group, part), device_id_type=MESH,
+        )
+
     for n in range(STEPS):
         step_loop(n)
-
-    def z_copy(to, origin):
-        return pltpu.make_async_remote_copy(
-            src_ref=z_out.at[to], dst_ref=z_in.at[pl.ds(SPAN * origin, SPAN)],
-            send_sem=z_send.at[to], recv_sem=z_recv.at[origin],
-            device_id=(LOCAL * to + group, part), device_id_type=MESH,
-        )
-
-    for step in FAR_FIRST:
-        z_copy(along(step), level).start()
     z_in[pl.ds(pl.multiple_of(SPAN * level, SPAN), SPAN)] = z_out[level]
-    for step in FAR_FIRST:
-        z_copy(level, along(step)).wait_recv()
 
     def out_copy(to, origin):
         return pltpu.make_async_remote_copy(
@@ -453,7 +468,15 @@
                 out_copy(b * PARTS + e, me).start()
         return carry
 
-    lax.fori_loop(0, PARTS, out_start, 0)
+    def windows_sent(k, carry):
+        window_copy(lax.rem(me + k, peers), me).wait_send()
+        return carry
+
+    lax.fori_loop(1, peers, windows_sent, 0)
+    for half in range(2):
+        for far in FAR_FIRST:
+            z_copy(level, along(far), half).wait_recv()
+        lax.fori_loop(half * PARTS // 2, (half + 1) * PARTS // 2, out_start, 0)
     landed[me] = outgoing_2[me]
 
     def out_wait(k, carry):
@@ -494,52 +517,43 @@
 
     zero = jnp.zeros((4, 8, LANES), F32)
     for q, total in enumerate(lax.fori_loop(0, LOCAL * near, add_up, (zero,) * near)):
-        totals[q] = total
+        totals[q] = total.reshape(OWN, LANES)
 
     def sum_copy(to, origin):
         return pltpu.make_async_remote_copy(
-            src_ref=totals.at[to], dst_ref=sums.at[origin],
+            src_ref=totals.at[to], dst_ref=sums.at[pl.ds(OWN * origin, OWN)],
             send_sem=s_send.at[to], recv_sem=s_recv.at[origin],
             device_id=(LOCAL * to + group, part), device_id_type=MESH,
         )
 
     for step in FAR_FIRST:
         sum_copy(along(step), level).start()
-    sums[level] = totals[level]
+    sums[pl.ds(pl.multiple_of(OWN * level, OWN), OWN)] = totals[level]
+
+    def outs_sent(k, carry):
+        out_copy(lax.rem(me + k, peers), me).wait_send()
+        return carry
+
+    lax.fori_loop(1, peers, outs_sent, 0)
+    for far in FAR_FIRST:
+        for half in range(2):
+            z_copy(along(far), level, half).wait_send()
     for step in FAR_FIRST:
         sum_copy(level, along(step)).wait_recv()
     for plane in range(4):
         for tile in range(4):
             for j in range(2):
-                for z in range(near):
-                    final[plane, tile, pl.ds(2 * z + j, 1)] = sums[z, tile, pl.ds(2 * plane + j, 1)]
+                final[plane, tile, pl.ds(j, near, stride=2)] = (
+                    sums[pl.ds(8 * tile + 2 * plane + j, near, stride=OWN)]
+                )
         speed = model[plane]
         total = jnp.concatenate([final[plane, tile] for tile in range(4)], axis=-1)
         scaling = (speed - lower_bound) * (upper_bound - speed) / (upper_bound - lower_bound)
         limit = barrier_weight / (upper_bound - speed) - barrier_weight / (speed - lower_bound)
         out[plane] = scaling * (total + limit)
 
-    for step in FAR_FIRST:
-        model_copy(along(step), level).wait_send()
-        rows_copy(along(step), level).wait_send()
-        z_copy(along(step), level).wait_send()
-        sum_copy(along(step), level).wait_send()
-
-    def ckpt_sent(k, carry):
-        to = lax.rem(part + k, PARTS)
-        ckpt_copy(0, to, part).wait_send()
-        ckpt_copy(1, to, part).wait_send()
-        return carry
-
-    lax.fori_loop(1, PARTS, ckpt_sent, 0)
-
-    def blocks_sent(k, carry):
-        to = lax.rem(me + k, peers)
-        window_copy(to, me).wait_send()
-        out_copy(to, me).wait_send()
-        return carry
-
-    lax.fori_loop(1, peers, blocks_sent, 0)
+    for far in FAR_FIRST:
+        sum_copy(along(far), level).wait_send()
 
 
 def on_device(near, model, offsets_x, offsets_y, ckpt_prev, ckpt_cur, wavelet, source, receivers, traces):
@@ -584,14 +598,14 @@
             pltpu.VMEM((peers, ROWS, LANES), F32),
             pltpu.VMEM((2, SPAN, LANES), F32),
             pltpu.VMEM((LOCAL * near, 6, 8, LANES), F32),
-            pltpu.VMEM((near, 4, 8, LANES), F32),
-            pltpu.VMEM((near, 4, 8, LANES), F32),
+            pltpu.VMEM((near, OWN, LANES), F32),
+            pltpu.VMEM((near * OWN, LANES), F32),
             pltpu.VMEM((4, 4, ROWS, LANES), F32),
             dma((5,)),
             dma((near,)), dma((near,)), dma((near,)), dma((near,)),
             dma((2, PARTS)), dma((2, PARTS)),
             dma((peers,)), dma((peers,)), dma((peers,)), dma((peers,)),
-            dma((near,)), dma((near,)), dma((near,)), dma((near,)),
+            dma((2, near)), dma((2, near)), dma((near,)), dma((near,)),
         ],
         compiler_params=pltpu.CompilerParams(
             collective_id=0, has_side_effects=True, vmem_limit_bytes=62 * 1024 * 1024

time: 68.4 us -> 63.9 us (0.934)
  the two profiles are of different devices: /device:TPU:1 before, /device:TPU:4 now
where the time goes in v4:
time: 63.9 us; the launch traced here: 63.6 us
  Pallas kernels  61.3 us (96%)
  local copies, waits for them, and re-layouts  1.57 us (2%)
  between operations  0.66 us (1%)
    pallas_call x1, Pallas kernels, on_device(): pl.pallas_call(functools.partial(kernel, near), out_shape=jax.ShapeDtypeS...  61.3 us
    unnamed x1, local copies, waits for them, and re-layouts  1.57 us

profile of v4, /device:TPU:4, one launch (start us, length us, event | category | flops | bytes accessed | tf_op | source)
XLA Modules:
  0.0 63.6 jit_solution(30090335463481410)
XLA Ops:
  0.7 61.3 %shard_map.91 = f32[4,16,512]{2,1,0:T(8,128)} custom-call(s32[32]{0:T(128)} %offx.1, s32[32]{0:T(128)} %offy.1, f32[1,4]{1,0:T(1,128)} %pulse.1, s32[1]{0:T(128)S(6)} %copy.11.place, f32[4,16,512]{2,1,0:T(8,128)} %model_in.1, f32[1,4,64,256]{3,2,1,0:T(8,128)} %prev_in.1, f32[1,4,64,256]{3,2,1,0:T(8,128)} %cur_in.1, s32[1,4096]{1,0:T(1,128)} %listing_in.1, ...), custom_call_target="tpu_custom_call" | custom-call | tf_op jit(solution)/shard_map/pallas_call | solution.py:566
  62.0 1.6 %copy.12 = f32[4,16,512]{2,1,0:T(8,128)} copy(f32[4,16,512]{2,1,0:T(8,128)} %shard_map.91) | data formatting | bytes 262144

commit v5 on v4

--- a/solution.py
+++ b/solution.py
@@ -27,11 +27,12 @@
 ROWS = 16
 HALO = 16
 OWN = 32
-CHUNK = 256
+CHUNK = 512
 PAD = 8
 FAR_FIRST = (4, 3, 5, 2, 6, 1, 7)
-FIRST = 4
-SECOND = 8
+PIECES = 2
+FIRST = 2
+SECOND = 4
 
 
 def iota(shape, dim):
@@ -124,12 +125,39 @@
         pl.semaphore_signal(barrier, inc=1, device_id=(LOCAL * along(step) + group, part), device_id_type=MESH)
     lax.fori_loop(1, peers, greet, 0)
 
-    make_bands(bands)
     inputs[0].wait()
     for to in range(near):
         for tile in range(4):
             for plane in range(4):
                 m_out[to, tile, pl.ds(2 * plane, 2)] = model[plane, pl.ds(2 * to, 2), pl.ds(LANES * tile, LANES)]
+    pl.semaphore_wait(barrier, peers - 1 + len(FAR_FIRST))
+
+    def model_copy(to, origin):
+        return pltpu.make_async_remote_copy(
+            src_ref=m_out.at[to], dst_ref=cyclic.at[origin],
+            send_sem=m_send.at[to], recv_sem=m_recv.at[origin],
+            device_id=(LOCAL * to + group, part), device_id_type=MESH,
+        )
+
+    def rows_copy(to, origin):
+        return pltpu.make_async_remote_copy(
+            src_ref=rows_out.at[to], dst_ref=rows_in.at[pl.ds(SPAN * origin, SPAN)],
+            send_sem=r_send.at[to], recv_sem=r_recv.at[origin],
+            device_id=(LOCAL * to + group, part), device_id_type=MESH,
+        )
+
+    def ckpt_copy(which, to, origin):
+        return pltpu.make_async_remote_copy(
+            src_ref=stage.at[which, to],
+            dst_ref=fields.at[which, pl.ds(2 + 2 * origin, 2), pl.ds(PAD, SPAN)],
+            send_sem=ck_send.at[which, to], recv_sem=ck_recv.at[which, origin],
+            device_id=(shot, to), device_id_type=MESH,
+        )
+
+    for step in FAR_FIRST:
+        model_copy(along(step), level).start()
+    cyclic[level] = m_out[level]
+
     for which, source in ((0, cur), (1, prev)):
         inputs[1 + which].wait()
         for i in range(2):
@@ -138,41 +166,13 @@
             for to in range(PARTS):
                 stage[which, to, i] = window(low, high, to)
 
-    pl.semaphore_wait(barrier, peers - 1 + len(FAR_FIRST))
-
-    def model_copy(to, origin):
-        return pltpu.make_async_remote_copy(
-            src_ref=m_out.at[to], dst_ref=cyclic.at[origin],
-            send_sem=m_send.at[to], recv_sem=m_recv.at[origin],
-            device_id=(LOCAL * to + group, part), device_id_type=MESH,
-        )
-
-    def rows_copy(to, origin):
-        return pltpu.make_async_remote_copy(
-            src_ref=rows_out.at[to], dst_ref=rows_in.at[pl.ds(SPAN * origin, SPAN)],
-            send_sem=r_send.at[to], recv_sem=r_recv.at[origin],
-            device_id=(LOCAL * to + group, part), device_id_type=MESH,
-        )
-
-    def ckpt_copy(which, to, origin):
-        return pltpu.make_async_remote_copy(
-            src_ref=stage.at[which, to],
-            dst_ref=fields.at[which, pl.ds(2 + 2 * origin, 2), pl.ds(PAD, SPAN)],
-            send_sem=ck_send.at[which, to], recv_sem=ck_recv.at[which, origin],
-            device_id=(shot, to), device_id_type=MESH,
-        )
-
-    for step in FAR_FIRST:
-        model_copy(along(step), level).start()
-    cyclic[level] = m_out[level]
-
-    def ckpt_start(k, carry):
-        to = lax.rem(part + k, PARTS)
-        ckpt_copy(0, to, part).start()
-        ckpt_copy(1, to, part).start()
-        return carry
-
-    lax.fori_loop(1, PARTS, ckpt_start, 0)
+        def ckpt_start(k, carry, which=which):
+            ckpt_copy(which, lax.rem(part + k, PARTS), part).start()
+            return carry
+
+        lax.fori_loop(1, PARTS, ckpt_start, 0)
+
+    make_bands(bands)
 
     for edge in (0, 1, PLANES + 2, PLANES + 3):
         for which in range(2):
@@ -426,10 +426,10 @@
         if n < STEPS - 1:
             lax.fori_loop(0, PARTS, step, 0)
             return
-        for half in range(2):
-            lax.fori_loop(half * PARTS // 2, (half + 1) * PARTS // 2, step, 0)
+        for piece in range(PIECES):
+            lax.fori_loop(piece * PARTS // PIECES, (piece + 1) * PARTS // PIECES, step, 0)
             for far in FAR_FIRST:
-                z_copy(along(far), level, half).start()
+                z_copy(along(far), level, piece).start()
 
     def send_parts(e, parts):
         both = jnp.where((lane & 63) < OWN, pltpu.roll(parts[0], LANES - HALO, 1), pltpu.roll(parts[1], OWN - HALO, 1))
@@ -440,11 +440,12 @@
             for j in range(2):
                 z_out[to, pl.ds(8 * e + 4 * j, 4)] = outgoing[e, pl.ds(2 * to + j, 4, stride=ROWS)]
 
-    def z_copy(to, origin, half):
+    def z_copy(to, origin, piece):
+        rows = SPAN // PIECES
         return pltpu.make_async_remote_copy(
-            src_ref=z_out.at[to, pl.ds(OWN * half, OWN)],
-            dst_ref=z_in.at[pl.ds(SPAN * origin + OWN * half, OWN)],
-            send_sem=z_send.at[half, to], recv_sem=z_recv.at[half, origin],
+            src_ref=z_out.at[to, pl.ds(rows * piece, rows)],
+            dst_ref=z_in.at[pl.ds(SPAN * origin + rows * piece, rows)],
+            send_sem=z_send.at[piece, to], recv_sem=z_recv.at[piece, origin],
             device_id=(LOCAL * to + group, part), device_id_type=MESH,
         )
 
@@ -473,10 +474,10 @@
         return carry
 
     lax.fori_loop(1, peers, windows_sent, 0)
-    for half in range(2):
+    for piece in range(PIECES):
         for far in FAR_FIRST:
-            z_copy(level, along(far), half).wait_recv()
-        lax.fori_loop(half * PARTS // 2, (half + 1) * PARTS // 2, out_start, 0)
+            z_copy(level, along(far), piece).wait_recv()
+        lax.fori_loop(piece * PARTS // PIECES, (piece + 1) * PARTS // PIECES, out_start, 0)
     landed[me] = outgoing_2[me]
 
     def out_wait(k, carry):
@@ -536,8 +537,8 @@
 
     lax.fori_loop(1, peers, outs_sent, 0)
     for far in FAR_FIRST:
-        for half in range(2):
-            z_copy(along(far), level, half).wait_send()
+        for piece in range(PIECES):
+            z_copy(along(far), level, piece).wait_send()
     for step in FAR_FIRST:
         sum_copy(level, along(step)).wait_recv()
     for plane in range(4):
@@ -605,7 +606,7 @@
             dma((near,)), dma((near,)), dma((near,)), dma((near,)),
             dma((2, PARTS)), dma((2, PARTS)),
             dma((peers,)), dma((peers,)), dma((peers,)), dma((peers,)),
-            dma((2, near)), dma((2, near)), dma((near,)), dma((near,)),
+            dma((PIECES, near)), dma((PIECES, near)), dma((near,)), dma((near,)),
         ],
         compiler_params=pltpu.CompilerParams(
             collective_id=0, has_side_effects=True, vmem_limit_bytes=62 * 1024 * 1024

time: 63.9 us -> 63.2 us (0.989)
  no operation moved by 1% of the time
where the time goes in v5:
time: 63.2 us; the launch traced here: 63 us
  Pallas kernels  60.8 us (96%)
  local copies, waits for them, and re-layouts  1.57 us (2%)
  between operations  0.66 us (1%)
    pallas_call x1, Pallas kernels, on_device(): pl.pallas_call(functools.partial(kernel, near), out_shape=jax.ShapeDtypeS...  60.8 us
    unnamed x1, local copies, waits for them, and re-layouts  1.57 us

profile of v5, /device:TPU:4, one launch (start us, length us, event | category | flops | bytes accessed | tf_op | source)
XLA Modules:
  0.0 63.0 jit_solution(10372263125365974243)
XLA Ops:
  0.7 60.8 %shard_map.91 = f32[4,16,512]{2,1,0:T(8,128)} custom-call(s32[32]{0:T(128)} %offx.1, s32[32]{0:T(128)} %offy.1, f32[1,4]{1,0:T(1,128)} %pulse.1, s32[1]{0:T(128)S(6)} %copy.11.place, f32[4,16,512]{2,1,0:T(8,128)} %model_in.1, f32[1,4,64,256]{3,2,1,0:T(8,128)} %prev_in.1, f32[1,4,64,256]{3,2,1,0:T(8,128)} %cur_in.1, s32[1,4096]{1,0:T(1,128)} %listing_in.1, ...), custom_call_target="tpu_custom_call" | custom-call | tf_op jit(solution)/shard_map/pallas_call | solution.py:567
  61.4 1.6 %copy.12 = f32[4,16,512]{2,1,0:T(8,128)} copy(f32[4,16,512]{2,1,0:T(8,128)} %shard_map.91) | data formatting | bytes 262144

commit v6 on v5

--- a/solution.py
+++ b/solution.py
@@ -84,7 +84,7 @@
     offx, offy, pulse, place, model_in, prev_in, cur_in, listing_in, record_in,
     out,
     model, prev, cur, listing, record,
-    m_out, cyclic, rows_out, rows_in, rows_16, stage, fields, lams, bands, along_y, halves, onto, summed_r, windows, arrived, speeds, c2v, first_lap,
+    m_out, cyclic, rows_out, rows_in, rows_16, stage, fields, lams, bands, along_y, halves, onto, summed_r, windows, arrived, doubled, speeds, c2v, first_lap,
     accels, partial, packed, outgoing, z_out, z_in, outgoing_2, landed, by_shot, placed, totals, sums, final,
     in_sems,
     m_send, m_recv, r_send, r_recv, ck_send, ck_recv, w_send, w_recv, o_send, o_recv,
@@ -358,23 +358,24 @@
 
     lax.fori_loop(0, PARTS, first, 0)
 
-    def window_wait(k, carry):
-        window_copy(me, lax.rem(me + k, peers)).wait_recv()
-        return carry
-
-    lax.fori_loop(1, peers, window_wait, 0)
-
     turn = offx[shot] & 63
 
-    def make_c2v(p, carry):
-        arrived[p, pl.ds(SPAN, SPAN)] = arrived[p, pl.ds(0, SPAN)]
-        speed = arrived[p, pl.ds(turn, SPAN)]
-        speeds[p] = speed
-        scaled = courant * speed
-        c2v[p] = scaled * scaled
-        return carry
-
-    lax.fori_loop(0, PLANES, make_c2v, 0)
+    def make_c2v(k):
+        e = lax.rem(part + k, PARTS)
+        for b in range(LOCAL):
+            @pl.when(b * PARTS + e != me)
+            def _():
+                window_copy(me, b * PARTS + e).wait_recv()
+        for i in range(2):
+            p = 2 * e + i
+            rows = arrived[p]
+            doubled[i, pl.ds(0, SPAN)] = rows
+            doubled[i, pl.ds(SPAN, SPAN)] = rows
+            speed = doubled[i, pl.ds(turn, SPAN)]
+            speeds[p] = speed
+            scaled = courant * speed
+            c2v[p] = scaled * scaled
+        return e
 
     flat = place[0]
     zc = lax.shift_right_logical(flat, 14)
@@ -397,6 +398,8 @@
                 prepare(lams, n, 1)
 
         def step(e, carry):
+            if not n:
+                e = make_c2v(e)
             laps = laplace(fields, now, 0, e) if n else [first_lap[0, 2 * e + i] for i in range(2)]
             accel = [accel_of(laps[i], 2 * e + i, n) for i in range(2)]
             if n < STEPS - 1:
@@ -480,15 +483,15 @@
         lax.fori_loop(piece * PARTS // PIECES, (piece + 1) * PARTS // PIECES, out_start, 0)
     landed[me] = outgoing_2[me]
 
-    def out_wait(k, carry):
-        out_copy(me, lax.rem(me + k, peers)).wait_recv()
-        return carry
-
-    lax.fori_loop(1, peers, out_wait, 0)
 
     group_of = lax.shift_right_logical(tile_lane, 5)
 
-    def put(b, carry):
+    def put(k, carry):
+        b = lax.rem(group + k, LOCAL)
+        for c in range(PARTS):
+            @pl.when(b * PARTS + c != me)
+            def _():
+                out_copy(me, b * PARTS + c).wait_recv()
         for j in range(2):
             for k in range(2):
                 pieces = [landed[b * PARTS + 4 * k + c, pl.ds(8 * j, 8)] for c in range(4)]
@@ -585,7 +588,8 @@
             pltpu.VMEM((STEPS * LANES, 2 * CHUNK), BF16),
             pltpu.VMEM((PLANES * SPAN, STEPS * LANES), F32),
             pltpu.VMEM((peers, 2, ROWS, LANES), F32),
-            pltpu.VMEM((PLANES, 2 * SPAN, LANES), F32),
+            pltpu.VMEM(plain, F32),
+            pltpu.VMEM((2, 2 * SPAN, LANES), F32),
             pltpu.VMEM(plain, F32),
             pltpu.VMEM(plain, F32),
             pltpu.VMEM((2,) + plain, F32),

time: 63.2 us -> 62.2 us (0.984)
  Pallas kernels: 60.8 us -> 59.9 us
    pallas_call x1, Pallas kernels: 60.8 us -> 59.9 us  [on_device(): pl.pallas_call(functools.partial(kernel, near), out_shape=jax.ShapeDtypeS...]
where the time goes in v6:
time: 62.2 us; the launch traced here: 62.1 us
  Pallas kernels  59.9 us (96%)
  local copies, waits for them, and re-layouts  1.57 us (3%)
  between operations  0.66 us (1%)
    pallas_call x1, Pallas kernels, on_device(): pl.pallas_call(functools.partial(kernel, near), out_shape=jax.ShapeDtypeS...  59.9 us
    unnamed x1, local copies, waits for them, and re-layouts  1.57 us

profile of v6, /device:TPU:4, one launch (start us, length us, event | category | flops | bytes accessed | tf_op | source)
XLA Modules:
  0.0 62.1 jit_solution(4264058293823315185)
XLA Ops:
  0.7 59.9 %shard_map.91 = f32[4,16,512]{2,1,0:T(8,128)} custom-call(s32[32]{0:T(128)} %offx.1, s32[32]{0:T(128)} %offy.1, f32[1,4]{1,0:T(1,128)} %pulse.1, s32[1]{0:T(128)S(6)} %copy.11.place, f32[4,16,512]{2,1,0:T(8,128)} %model_in.1, f32[1,4,64,256]{3,2,1,0:T(8,128)} %prev_in.1, f32[1,4,64,256]{3,2,1,0:T(8,128)} %cur_in.1, s32[1,4096]{1,0:T(1,128)} %listing_in.1, ...), custom_call_target="tpu_custom_call" | custom-call | tf_op jit(solution)/shard_map/pallas_call | solution.py:570
  60.5 1.6 %copy.12 = f32[4,16,512]{2,1,0:T(8,128)} copy(f32[4,16,512]{2,1,0:T(8,128)} %shard_map.91) | data formatting | bytes 262144

commit v7 on v6

--- a/solution.py
+++ b/solution.py
@@ -271,8 +271,8 @@
                         rows_in[pl.ds(8 * (2 * b + k) + 2 * plane + j, 8, stride=SPAN)]
                     )
         for i in range(2):
-            low = [rows_16[i, k] for k in range(2)]
-            high = [pltpu.roll(rows_16[2 + i, k], 64, 1) for k in range(2)]
+            low = [rows_16[i, k, pl.ds(0, ROWS)] for k in range(2)]
+            high = [pltpu.roll(rows_16[2 + i, k, pl.ds(0, ROWS)], 64, 1) for k in range(2)]
             for to in range(PARTS):
                 windows[b * PARTS + to, i] = window(low, high, to)
         for to in range(PARTS):
@@ -328,13 +328,14 @@
 
     lax.fori_loop(0, PLANES, to_lam, 0)
 
-    def ckpt_wait(k, carry):
-        origin = lax.rem(part + k, PARTS)
-        ckpt_copy(0, part, origin).wait_recv()
-        ckpt_copy(1, part, origin).wait_recv()
-        return carry
-
-    lax.fori_loop(1, PARTS, ckpt_wait, 0)
+    def ckpt_wait(which):
+        def one(k, carry):
+            ckpt_copy(which, part, lax.rem(part + k, PARTS)).wait_recv()
+            return carry
+
+        lax.fori_loop(1, PARTS, one, 0)
+
+    ckpt_wait(0)
 
     def ckpt_sent(k, carry):
         to = lax.rem(part + k, PARTS)
@@ -342,21 +343,22 @@
         ckpt_copy(1, to, part).wait_send()
         return carry
 
+    prepare(fields, 0, 0)
+    prepare(lams, 0, 1)
+
+    def first(e, carry):
+        for which, field in ((0, fields), (1, lams)):
+            for i, value in enumerate(laplace(field, 0, which, e)):
+                first_lap[which, 2 * e + i] = value
+        return carry
+
+    lax.fori_loop(0, PARTS, first, 0)
+
+    ckpt_wait(1)
     lax.fori_loop(1, PARTS, ckpt_sent, 0)
     for far in FAR_FIRST:
         model_copy(along(far), level).wait_send()
         rows_copy(along(far), level).wait_send()
-
-    prepare(fields, 0, 0)
-    prepare(lams, 0, 1)
-
-    def first(e, carry):
-        for which, field in ((0, fields), (1, lams)):
-            for i, value in enumerate(laplace(field, 0, which, e)):
-                first_lap[which, 2 * e + i] = value
-        return carry
-
-    lax.fori_loop(0, PARTS, first, 0)
 
     turn = offx[shot] & 63
 
@@ -438,7 +440,7 @@
         both = jnp.where((lane & 63) < OWN, pltpu.roll(parts[0], LANES - HALO, 1), pltpu.roll(parts[1], OWN - HALO, 1))
         packed[e, pl.ds(0, SPAN)] = both
         packed[e, pl.ds(SPAN, SPAN)] = both
-        outgoing[e] = packed[e, pl.ds((SPAN - turn) & 63, SPAN)]
+        outgoing[e, pl.ds(0, SPAN)] = packed[e, pl.ds((SPAN - turn) & 63, SPAN)]
         for to in range(near):
             for j in range(2):
                 z_out[to, pl.ds(8 * e + 4 * j, 4)] = outgoing[e, pl.ds(2 * to + j, 4, stride=ROWS)]
@@ -551,7 +553,7 @@
                     sums[pl.ds(8 * tile + 2 * plane + j, near, stride=OWN)]
                 )
         speed = model[plane]
-        total = jnp.concatenate([final[plane, tile] for tile in range(4)], axis=-1)
+        total = jnp.concatenate([final[plane, tile, pl.ds(0, ROWS)] for tile in range(4)], axis=-1)
         scaling = (speed - lower_bound) * (upper_bound - speed) / (upper_bound - lower_bound)
         limit = barrier_weight / (upper_bound - speed) - barrier_weight / (speed - lower_bound)
         out[plane] = scaling * (total + limit)
@@ -577,8 +579,8 @@
             pltpu.VMEM((near, 4, 8, LANES), F32),
             pltpu.VMEM((near, 4, 8, LANES), F32),
             pltpu.VMEM((near, SPAN, LANES), F32),
-            pltpu.VMEM((near * SPAN, LANES), F32),
-            pltpu.VMEM((4, 2, ROWS, LANES), F32),
+            pltpu.VMEM((near * SPAN + SPAN, LANES), F32),
+            pltpu.VMEM((4, 2, ROWS + PAD, LANES), F32),
             pltpu.VMEM((2, PARTS, 2, SPAN, LANES), F32),
             pltpu.VMEM((2,) + padded, F32),
             pltpu.VMEM((3,) + padded, F32),
@@ -596,16 +598,16 @@
             pltpu.VMEM((2,) + plain, F32),
             pltpu.VMEM(plain, F32),
             pltpu.VMEM((PARTS, 2 * SPAN, LANES), F32),
-            pltpu.VMEM((PARTS, SPAN, LANES), F32),
+            pltpu.VMEM((PARTS, SPAN + ROWS, LANES), F32),
             pltpu.VMEM((near, SPAN, LANES), F32),
-            pltpu.VMEM((near * SPAN, LANES), F32),
+            pltpu.VMEM((near * SPAN + SPAN, LANES), F32),
             pltpu.VMEM((peers, ROWS, LANES), F32),
             pltpu.VMEM((peers, ROWS, LANES), F32),
-            pltpu.VMEM((2, SPAN, LANES), F32),
+            pltpu.VMEM((2, SPAN + PAD, LANES), F32),
             pltpu.VMEM((LOCAL * near, 6, 8, LANES), F32),
             pltpu.VMEM((near, OWN, LANES), F32),
-            pltpu.VMEM((near * OWN, LANES), F32),
-            pltpu.VMEM((4, 4, ROWS, LANES), F32),
+            pltpu.VMEM((near * OWN + OWN, LANES), F32),
+            pltpu.VMEM((4, 4, ROWS + PAD, LANES), F32),
             dma((5,)),
             dma((near,)), dma((near,)), dma((near,)), dma((near,)),
             dma((2, PARTS)), dma((2, PARTS)),

time: 62.2 us -> 62.2 us (level)
  no operation moved by 1% of the time
where the time goes in v7:
time: 62.2 us; the launch traced here: 62.1 us
  Pallas kernels  59.9 us (96%)
  local copies, waits for them, and re-layouts  1.57 us (3%)
  between operations  0.66 us (1%)
    pallas_call x1, Pallas kernels, on_device(): pl.pallas_call(functools.partial(kernel, near), out_shape=jax.ShapeDtypeS...  59.9 us
    unnamed x1, local copies, waits for them, and re-layouts  1.57 us

profile of v7, /device:TPU:4, one launch (start us, length us, event | category | flops | bytes accessed | tf_op | source)
XLA Modules:
  0.0 62.1 jit_solution(8165823420943222528)
XLA Ops:
  0.7 59.9 %shard_map.91 = f32[4,16,512]{2,1,0:T(8,128)} custom-call(s32[32]{0:T(128)} %offx.1, s32[32]{0:T(128)} %offy.1, f32[1,4]{1,0:T(1,128)} %pulse.1, s32[1]{0:T(128)S(6)} %copy.11.place, f32[4,16,512]{2,1,0:T(8,128)} %model_in.1, f32[1,4,64,256]{3,2,1,0:T(8,128)} %prev_in.1, f32[1,4,64,256]{3,2,1,0:T(8,128)} %cur_in.1, s32[1,4096]{1,0:T(1,128)} %listing_in.1, ...), custom_call_target="tpu_custom_call" | custom-call | tf_op jit(solution)/shard_map/pallas_call | solution.py:572
  60.5 1.6 %copy.12 = f32[4,16,512]{2,1,0:T(8,128)} copy(f32[4,16,512]{2,1,0:T(8,128)} %shard_map.91) | data formatting | bytes 262144

commit v8 on v7

--- a/solution.py
+++ b/solution.py
@@ -30,7 +30,7 @@
 CHUNK = 512
 PAD = 8
 FAR_FIRST = (4, 3, 5, 2, 6, 1, 7)
-PIECES = 2
+PIECES = 4
 FIRST = 2
 SECOND = 4
 

time: 62.2 us -> 62.3 us (level); the launches traced: 62.1 us -> 61.2 us
  Pallas kernels: 59.9 us -> 59 us
    pallas_call x1, Pallas kernels: 59.9 us -> 59 us  [on_device(): pl.pallas_call(functools.partial(kernel, near), out_shape=jax.ShapeDtypeS...]
where the time goes in v8:
time: 62.3 us; the launch traced here: 61.2 us
  Pallas kernels  59 us (95%)
  local copies, waits for them, and re-layouts  1.57 us (3%)
  between operations  0.66 us (1%)
    pallas_call x1, Pallas kernels, on_device(): pl.pallas_call(functools.partial(kernel, near), out_shape=jax.ShapeDtypeS...  59 us
    unnamed x1, local copies, waits for them, and re-layouts  1.57 us

profile of v8, /device:TPU:4, one launch (start us, length us, event | category | flops | bytes accessed | tf_op | source)
XLA Modules:
  0.0 61.2 jit_solution(7038666714528251848)
XLA Ops:
  0.7 59.0 %shard_map.91 = f32[4,16,512]{2,1,0:T(8,128)} custom-call(s32[32]{0:T(128)} %offx.1, s32[32]{0:T(128)} %offy.1, f32[1,4]{1,0:T(1,128)} %pulse.1, s32[1]{0:T(128)S(6)} %copy.11.place, f32[4,16,512]{2,1,0:T(8,128)} %model_in.1, f32[1,4,64,256]{3,2,1,0:T(8,128)} %prev_in.1, f32[1,4,64,256]{3,2,1,0:T(8,128)} %cur_in.1, s32[1,4096]{1,0:T(1,128)} %listing_in.1, ...), custom_call_target="tpu_custom_call" | custom-call | tf_op jit(solution)/shard_map/pallas_call | solution.py:572
  59.6 1.6 %copy.12 = f32[4,16,512]{2,1,0:T(8,128)} copy(f32[4,16,512]{2,1,0:T(8,128)} %shard_map.91) | data formatting | bytes 262144
